TPU v7x, 32 devices: a whole 2x2x4 slice. The times are simulated.
32 devices in a mesh: groups: 2 (over y), expert: 8 (over z, x), mp: 2 (over core).
Axes of the slice: x: 2, y: 2, z: 4, core: 2. Of those that a mesh axis runs over, the one named last changes fastest.
Arguments:
- tokens: bfloat16 [1024, 6144], P(('groups', 'expert'), 'mp'), parts along dimension 0, may hold values from -6 to 6
- expert_ids: int32 [1024, 2], P(('groups', 'expert')), parts along dimension 0, may hold values from 0 to 7, all different within a row; in each aligned block of 64 rows (0 to 63, 64 to 127, ...) at most 24 rows name the same one
- gate_ranks: int32 [1024, 2], P(('groups', 'expert')), parts along dimension 0, may hold values from 1 to 256
- limits: int32 [16, 8], P(('groups', 'expert')), parts along dimension 0, may hold values from 12 to 24
- w_in: bfloat16 [8, 6144, 2, 4096], P('expert', None, None, 'mp'), may hold values from -0.078125 to 0.078125
- w_out: bfloat16 [8, 4096, 6144], P('expert', 'mp'), may hold values from -0.0625 to 0.0625
Outputs:
- mixed: bfloat16 [1024, 6144], P(('groups', 'expert'), 'mp'), parts along dimension 0
There are 2 independent parts, one for each index of `groups`. A program takes and returns all parts, laid end to end along the dimension named above; an argument that names none is the same for every part. Nothing has to cross between parts.
Inputs may be any that keep to these rules, and one draw needn't show every extreme that they name: `expert_ids`: within one block of 64 rows (the tokens of one index of expert) no expert is named by more than 24 picks; the two picks of a token differ.
All inputs are finite; a program needn't handle non-finite values.
Results may differ from a plain program's by a relative error of at most 0.0058.
Values may be sent and summed in bfloat16 or wider, within the bound.
A program may use at most 320 MiB of HBM per device.

v0:
```python
import jax
import jax.numpy as jnp
from jax import lax
from jax.sharding import PartitionSpec as P

D = 6144
NUM_EXPERTS = 8
EXP_WIN = 4
CAP = 24


def on_device(tokens, expert_ids, gate_ranks, limits, w_in, w_out):
    tok_dev = expert_ids.shape[0]
    slot_count = lax.axis_size("expert")
    slices = slot_count // EXP_WIN
    hid_local = w_in.shape[3]
    chosen = expert_ids.reshape(-1)
    labels = jnp.arange(NUM_EXPERTS, dtype=jnp.int32)
    onehot = (chosen[:, None] == labels[None, :]).astype(jnp.int32)
    before = jnp.cumsum(onehot, axis=0) - onehot
    position = jnp.sum(before * onehot, axis=1)
    limit_of = jnp.sum(onehot * limits[0][None, :], axis=1)
    keep_mask = (chosen < EXP_WIN) & (position < limit_of)
    rank_vals = gate_ranks.astype(jnp.float32)
    gate_share = (rank_vals / jnp.sum(rank_vals, axis=1, keepdims=True)).reshape(-1)
    slot_index = chosen * CAP + position
    columns = jnp.arange(EXP_WIN * CAP, dtype=jnp.int32)
    select = (keep_mask[:, None] & (slot_index[:, None] == columns[None, :])).astype(jnp.float32)
    owners = (
        (jnp.arange(tok_dev * 2, dtype=jnp.int32) // 2)[:, None]
        == jnp.arange(tok_dev, dtype=jnp.int32)[None, :]
    ).astype(jnp.float32)
    pick_matrix = jnp.dot(select.T, owners, preferred_element_type=jnp.float32).astype(jnp.bfloat16)
    pick_slots = jnp.broadcast_to(
        pick_matrix.reshape(EXP_WIN, 1, CAP, tok_dev), (EXP_WIN, slices, CAP, tok_dev)
    ).reshape(slot_count * CAP, tok_dev)
    combine = jnp.dot(
        owners.T,
        select * gate_share[:, None],
        preferred_element_type=jnp.float32,
        precision=lax.Precision.HIGHEST,
    )
    combine_slots = jnp.broadcast_to(
        combine.reshape(tok_dev, EXP_WIN, 1, CAP), (tok_dev, EXP_WIN, slices, CAP)
    ).reshape(tok_dev, slot_count * CAP)
    source = lax.all_gather(tokens, "mp", axis=1, tiled=True)
    width = source.shape[1]
    outgoing = jnp.dot(pick_slots, source, preferred_element_type=jnp.float32).astype(jnp.bfloat16)
    outgoing = outgoing.reshape(slot_count, CAP, width)
    received = lax.all_to_all(outgoing, "expert", split_axis=0, concat_axis=0, tiled=True)
    senders = received.shape[0]
    depth = received.shape[1]
    flat_rows = received.reshape(senders * depth, D)
    gate_up = jnp.dot(
        flat_rows, w_in[0].reshape(D, 2 * hid_local), preferred_element_type=jnp.float32
    )
    gate_up = gate_up.reshape(senders * depth, 2, hid_local)
    hidden = (jax.nn.silu(gate_up[:, 0]) * gate_up[:, 1]).astype(jnp.bfloat16)
    partial_value = jnp.dot(hidden, w_out[0], preferred_element_type=jnp.float32).reshape(
        senders, depth, D
    )
    core_share = lax.psum_scatter(partial_value, "mp", scatter_dimension=2, tiled=True).astype(
        jnp.bfloat16
    )
    returned = lax.all_to_all(core_share, "expert", split_axis=0, concat_axis=0, tiled=True)
    half_width = returned.shape[2]
    slot_rows_all = returned.reshape(slot_count * CAP, half_width).astype(jnp.float32)
    mixed_out = jnp.dot(
        combine_slots,
        slot_rows_all,
        preferred_element_type=jnp.float32,
        precision=lax.Precision.HIGHEST,
    )
    return mixed_out.astype(jnp.bfloat16)


def solution(mesh):
    placed = (
        P(("groups", "expert"), "mp"),
        P(("groups", "expert"), None),
        P(("groups", "expert"), None),
        P(("groups", "expert"), None),
        P("expert", None, None, "mp"),
        P("expert", "mp", None),
    )
    return jax.shard_map(
        on_device,
        mesh=mesh,
        in_specs=placed,
        out_specs=P(("groups", "expert"), "mp"),
        check_vma=False,
    )
```

profile of v0, /device:TPU:0, one launch (start us, length us, event | category | flops | bytes accessed | tf_op | source)
XLA Modules:
  0.0 216.9 jit_solution(8550022322892864854)
XLA Ops:
  6.5 0.8 copy.11
  7.3 0.1 reshape.64
  7.4 0.1 fusion.5
  7.5 0.2 reduce_window_sum.11
  7.7 0.8 select_reduce_fusion
  8.6 0.3 convolution_convert_fusion.2
  8.8 0.1 copy.14
  9.0 2.7 %all_gather.3 = bf16[64,6144]{1,0:T(8,128)(2,1)S(1)} all-gather(bf16[64,3072]{1,0:T(8,128)(2,1)} %param.6), channel_id=1, replica_groups=mesh['groups'=2,'expert'=8,'mp'=2] {'mp'}, dimensions={1}, use_global_device_ids=true | all-gather | bytes 1179648 | tf_op jit(solution)/shard_map/all_gather | solution.py:46
  11.6 2.2 convolution_convert_fusion
  13.8 7.2 %all-to-all-start = ((bf16[8,24,6144]{2,1,0:T(8,128)(2,1)}), bf16[8,24,6144]{2,1,0:T(8,128)(2,1)S(1)}, u32[]{:S(2)}, u32[]{:S(2)}) async-start(bf16[8,24,6144]{2,1,0:T(8,128)(2,1)} %bitcast.5), calls=%async_computation | async-start | bytes 4718592 | tf_op jit(solution)/shard_map/all_to_all | solution.py:50
  21.0 33.3 %copy.17 = bf16[768,8,2,2048]{3,1,2,0:T(8,128)(2,1)} copy(bf16[768,8,2,2048]{3,2,1,0:T(2,128)(2,1)} %bitcast.29) | data formatting | bytes 100663296
  54.3 64.7 %copy.15 = bf16[4096,6144]{1,0:T(8,128)(2,1)} copy(bf16[4096,6144]{0,1:T(8,128)(2,1)} %bitcast.28) | data formatting | bytes 100663296 | tf_op jit(solution)/shard_map/dot_general | solution.py:54
  119.0 1.4 copy-done
  120.4 22.8 %fusion.18 = f32[192,2,2048]{2,0,1:T(8,128)S(1)} fusion(bf16[192,6144,1]{1,0,2:T(8,128)(2,1)} %bitcast.32, bf16[2,2048,6144]{2,1,0:T(8,128)(2,1)} %bitcast.30), kind=kOutput, calls=%fused_computation.33 | convolution fusion | flops 9663676416 | bytes 55836672 | tf_op jit(solution)/shard_map/dot_general | solution.py:54
  143.2 0.4 fusion.2
  143.7 12.9 %fusion = f32[8,24,6144]{2,1,0:T(8,128)} fusion(bf16[8,24,2048]{2,1,0:T(8,128)(2,1)S(1)} %bitcast.33, bf16[1,2048,6144]{2,1,0:T(8,128)(2,1)} %param.11), kind=kOutput, calls=%fused_computation | convolution fusion | flops 4831838208 | bytes 30670848 | tf_op jit(solution)/shard_map/dot_general | solution.py:59
  156.6 14.1 %reduce-scatter.2.cloned.1.call-done = f32[8,24,3072]{2,1,0:T(8,128)} async-done(((f32[8,24,6144]{2,1,0:T(8,128)}), f32[8,24,3072]{2,1,0:T(8,128)}) %reduce-scatter.2.cloned.1.call-update) | async-done | bytes 2359312 | tf_op jit(solution)/shard_map/reduce_scatter | solution.py:62
  170.8 2.8 %convert_element_type.34 = bf16[8,24,3072]{2,1,0:T(8,128)(2,1)} convert(f32[8,24,3072]{2,1,0:T(8,128)} %reduce-scatter.2.cloned.1.call-done) | non-fusion elementwise | flops 589824 | bytes 3538944 | tf_op jit(solution)/shard_map/convert_element_type | solution.py:62
  173.6 5.7 %all-to-all-start.1 = ((bf16[8,24,3072]{2,1,0:T(8,128)(2,1)}), bf16[8,24,3072]{2,1,0:T(8,128)(2,1)S(1)}, u32[]{:S(2)}, u32[]{:S(2)}) async-start(bf16[8,24,3072]{2,1,0:T(8,128)(2,1)} %convert_element_type.34), calls=%async_computation.2 | async-start | bytes 2359296 | tf_op jit(solution)/shard_map/all_to_all | solution.py:65
  179.4 0.1 copy.12
  179.5 0.1 mul.50
  179.6 0.3 fusion.3
  180.0 28.5 %all-to-all-done.1 = bf16[8,24,3072]{2,1,0:T(8,128)(2,1)S(1)} async-done(((bf16[8,24,3072]{2,1,0:T(8,128)(2,1)}), bf16[8,24,3072]{2,1,0:T(8,128)(2,1)S(1)}, u32[]{:S(2)}, u32[]{:S(2)}) %all-to-all-start.1) | async-done | bytes 1179680 | tf_op jit(solution)/shard_map/all_to_all | solution.py:65
  208.4 1.6 convolution_convert_fusion.1
  (12 shorter events, 0.1 us)
Async XLA Ops:
  13.8 105.2 %all-to-all-start = ((bf16[8,24,6144]{2,1,0:T(8,128)(2,1)}), bf16[8,24,6144]{2,1,0:T(8,128)(2,1)S(1)}, u32[]{:S(2)}, u32[]{:S(2)}) async-start(bf16[8,24,6144]{2,1,0:T(8,128)(2,1)} %bitcast.5), calls=%async_computation | async-start | bytes 4718592 | tf_op jit(solution)/shard_map/all_to_all | solution.py:50
  21.0 149.8 %reduce-scatter.2.cloned.1.call-start = ((), (), s32[]{:S(2)}) async-start(), calls=%async_computation.3 | async-start | bytes 7077888 | tf_op jit(solution)/shard_map/reduce_scatter | solution.py:62
  119.0 1.4 copy-start
  156.6 22.7 %copy-start.1 = (s32[64,2]{0,1:T(2,128)S(1)}, s32[64,2]{0,1:T(2,128)}, u32[]{:S(2)}) copy-start(s32[64,2]{0,1:T(2,128)} %param.8) | copy-start | bytes 1540
  173.6 34.8 %all-to-all-start.1 = ((bf16[8,24,3072]{2,1,0:T(8,128)(2,1)}), bf16[8,24,3072]{2,1,0:T(8,128)(2,1)S(1)}, u32[]{:S(2)}, u32[]{:S(2)}) async-start(bf16[8,24,3072]{2,1,0:T(8,128)(2,1)} %convert_element_type.34), calls=%async_computation.2 | async-start | bytes 2359296 | tf_op jit(solution)/shard_map/all_to_all | solution.py:65
Sparse Core Ops, SparseCore 0:
  156.7 13.9 reduce-scatter.1
where the time goes:
time: 219 us; the launch traced here: 217 us
  local copies, waits for them, and re-layouts  101 us (46%)
  waiting for transfers between devices  42.6 us (19%)
  matrix products  40 us (18%)
  between operations  13.5 us (6%)
  starting transfers between devices  13 us (6%)
  other arithmetic  4.41 us (2%)
  blocking collectives  2.66 us (1%)
    dot_general x1, local copies, waits for them, and re-layouts, on_device(): jnp.dot(flat_rows, w_in[0].reshape(D, 2 * hid_local), preferred_element_t...  64.7 us
    unnamed x6, local copies, waits for them, and re-layouts  35.5 us
    all_to_all x1, waiting for transfers between devices, on_device(): lax.all_to_all(core_share, 'expert', split_axis=0, concat_axis=0, tiled=T...  28.5 us
    dot_general x1, matrix products, on_device(): jnp.dot(flat_rows, w_in[0].reshape(D, 2 * hid_local), preferred_element_t...  22.8 us
    reduce_scatter x1, waiting for transfers between devices, on_device(): lax.psum_scatter(partial_value, 'mp', scatter_dimension=2, tiled=True)  14.1 us
    dot_general x1, matrix products, on_device(): jnp.dot(hidden, w_out[0], preferred_element_type=jnp.float32)  12.9 us
    all_to_all x1, starting transfers between devices, on_device(): lax.all_to_all(outgoing, 'expert', split_axis=0, concat_axis=0, tiled=True)  7.17 us
    all_to_all x1, starting transfers between devices, on_device(): lax.all_to_all(core_share, 'expert', split_axis=0, concat_axis=0, tiled=T...  5.74 us
  transfers between devices with their start and end apart: 3, of which 2 were waited for; matrix products, arithmetic and copies ran while one was open for 45% of the time, Pallas kernels for 0%

commit v1 on v0

v1 whole, which is shorter than its diff:
```python
import functools
import jax
import jax.numpy as jnp
from jax import lax
from jax.experimental import pallas as pl
from jax.experimental.pallas import tpu as pltpu
from jax.sharding import PartitionSpec as P

D = 6144
NUM_EXPERTS = 8
EXP_WIN = 4
CAP = 24

CHUNKS = 1
STEP = 512
COLS = 512


def gate_up_body(steps, first, last, *refs):
    if first:
        x_ref, w_ref, o_ref, *rest = refs
    else:
        x_ref, w_ref, before_ref, o_ref, *rest = refs
    sums = rest[0] if last else o_ref
    step = pl.program_id(0)

    @pl.when(step == 0)
    def _():
        sums[...] = jnp.zeros_like(sums) if first else before_ref[...]

    depth = w_ref.shape[0]
    rows = x_ref.shape[0] * x_ref.shape[1]
    x = x_ref[...].reshape(rows, depth)
    w = w_ref[...].reshape(depth, sums.shape[1])
    sums[...] += jnp.dot(x, w, preferred_element_type=jnp.float32)

    if last:
        @pl.when(step == steps - 1)
        def _():
            for j in range(o_ref.shape[1] // 128):
                gate = sums[:, 256 * j:256 * j + 128]
                up = sums[:, 256 * j + 128:256 * j + 256]
                o_ref[:, 128 * j:128 * j + 128] = (gate * jax.nn.sigmoid(gate) * up).astype(o_ref.dtype)


def gate_up(x, w, before, chunk, last):
    ranks, halves, depth, width = x.shape
    rows = ranks * depth
    wide = w.shape[1] * 128
    per_half = width // STEP
    half = w.shape[0] // halves // STEP
    steps = halves * per_half
    first = before is None
    in_specs = [
        pl.BlockSpec((ranks, None, depth, STEP), lambda k: (0, k // per_half, 0, k % per_half)),
        pl.BlockSpec((STEP, w.shape[1], 128),
                     lambda k: (k // per_half * half + chunk * per_half + k % per_half, 0, 0)),
    ]
    if not first:
        in_specs.append(pl.BlockSpec((rows, wide), lambda k: (0, 0)))
    out = jax.ShapeDtypeStruct((rows, wide // 2), jnp.bfloat16) if last else jax.ShapeDtypeStruct((rows, wide), jnp.float32)
    return pl.pallas_call(
        functools.partial(gate_up_body, steps, first, last),
        grid=(steps,),
        in_specs=in_specs,
        out_specs=pl.BlockSpec(out.shape, lambda k: (0, 0)),
        out_shape=out,
        scratch_shapes=[pltpu.VMEM((rows, wide), jnp.float32)] if last else [],
        compiler_params=pltpu.CompilerParams(vmem_limit_bytes=48 * 2**20),
        cost_estimate=pl.CostEstimate(flops=2 * rows * halves * width * wide, bytes_accessed=halves * width * wide * 2, transcendentals=0),
    )(*([x, w] if first else [x, w, before]))


def down_body(at_ref, h_ref, w_ref, o_ref):
    o_ref[...] = jnp.dot(h_ref[...], w_ref[...], preferred_element_type=jnp.float32).astype(o_ref.dtype)


def down(hidden, w, at, width, kind):
    rows, depth = hidden.shape
    return pl.pallas_call(
        down_body,
        grid_spec=pltpu.PrefetchScalarGridSpec(
            num_scalar_prefetch=1,
            grid=(width // COLS,),
            in_specs=[
                pl.BlockSpec((rows, depth), lambda k, at: (0, 0)),
                pl.BlockSpec((depth, COLS), lambda k, at: (0, at[0] + k)),
            ],
            out_specs=pl.BlockSpec((rows, COLS), lambda k, at: (0, k)),
        ),
        out_shape=jax.ShapeDtypeStruct((rows, width), kind),
        compiler_params=pltpu.CompilerParams(vmem_limit_bytes=48 * 2**20),
        cost_estimate=pl.CostEstimate(flops=2 * rows * depth * width, bytes_accessed=depth * width * 2, transcendentals=0),
    )(at.reshape(1), hidden, w)


def on_device(tokens, expert_ids, gate_ranks, limits, w_in, w_out):
    tok_dev = expert_ids.shape[0]
    slot_count = lax.axis_size("expert")
    slices = slot_count // EXP_WIN
    hid_local = w_in.shape[3]
    chosen = expert_ids.reshape(-1)
    labels = jnp.arange(NUM_EXPERTS, dtype=jnp.int32)
    onehot = (chosen[:, None] == labels[None, :]).astype(jnp.int32)
    before = jnp.cumsum(onehot, axis=0) - onehot
    position = jnp.sum(before * onehot, axis=1)
    limit_of = jnp.sum(onehot * limits[0][None, :], axis=1)
    keep_mask = (chosen < EXP_WIN) & (position < limit_of)
    rank_vals = gate_ranks.astype(jnp.float32)
    gate_share = (rank_vals / jnp.sum(rank_vals, axis=1, keepdims=True)).reshape(-1)
    slot_index = chosen * CAP + position
    columns = jnp.arange(EXP_WIN * CAP, dtype=jnp.int32)
    select = (keep_mask[:, None] & (slot_index[:, None] == columns[None, :])).astype(jnp.float32)
    owners = (
        (jnp.arange(tok_dev * 2, dtype=jnp.int32) // 2)[:, None]
        == jnp.arange(tok_dev, dtype=jnp.int32)[None, :]
    ).astype(jnp.float32)
    pick_matrix = jnp.dot(select.T, owners, preferred_element_type=jnp.float32).astype(jnp.bfloat16)
    combine = jnp.dot(
        owners.T,
        select * gate_share[:, None],
        preferred_element_type=jnp.float32,
        precision=lax.Precision.HIGHEST,
    )
    half = tokens.shape[1]
    width = half // CHUNKS
    same_rank = [[e * slices + r for e in range(EXP_WIN)] for r in range(slices)]
    same_expert = [[e * slices + r for r in range(slices)] for e in range(EXP_WIN)]
    core = lax.axis_index("mp")
    weights = w_in[0].reshape(D, 2, hid_local // 128, 128).transpose(0, 2, 1, 3)
    weights = weights.reshape(D, hid_local // 64, 128)

    sums = None
    for c in range(CHUNKS):
        part = tokens[:, c * width:(c + 1) * width]
        outgoing = jnp.dot(pick_matrix, part, preferred_element_type=jnp.float32).astype(jnp.bfloat16)
        outgoing = outgoing.reshape(EXP_WIN, CAP, width)
        arrived = lax.all_to_all(
            outgoing, "expert", split_axis=0, concat_axis=0, axis_index_groups=same_rank, tiled=True
        ).reshape(EXP_WIN * CAP, width)
        pairs = [[2 * i + m for i in group for m in range(2)] for group in same_expert]
        rows = lax.all_gather(arrived, ("expert", "mp"), axis_index_groups=pairs)
        rows = rows.reshape(slices, 2, EXP_WIN * CAP, width)
        sums = gate_up(rows, weights, sums, c, c == CHUNKS - 1)
    hidden = sums

    mixed = []
    for c in range(CHUNKS):
        tiles = half // COLS
        start = c * (width // COLS)
        theirs = down(hidden, w_out[0], (1 - core) * tiles + start, width, jnp.bfloat16)
        landed = lax.ppermute(theirs, "mp", [(0, 1), (1, 0)])
        mine = down(hidden, w_out[0], core * tiles + start, width, jnp.float32)
        share = (mine + landed.astype(jnp.float32)).astype(jnp.bfloat16)
        share = share.reshape(slices, EXP_WIN * CAP, width)
        rank = lax.rem(lax.axis_index("expert"), slices)
        total = lax.dynamic_index_in_dim(share, rank, 0, False).astype(jnp.float32)
        for d in range(1, slices):
            sent = lax.dynamic_index_in_dim(share, lax.rem(rank + d, slices), 0, False)
            ring = [(g[r], g[(r + d) % slices]) for g in same_expert for r in range(slices)]
            total = total + lax.ppermute(sent, "expert", ring).astype(jnp.float32)
        total = total.astype(jnp.bfloat16).reshape(EXP_WIN, CAP, width)
        returned = lax.all_to_all(
            total, "expert", split_axis=0, concat_axis=0, axis_index_groups=same_rank, tiled=True
        ).reshape(EXP_WIN * CAP, width)
        mixed.append(jnp.dot(
            combine,
            returned.astype(jnp.float32),
            preferred_element_type=jnp.float32,
            precision=lax.Precision.HIGHEST,
        ).astype(jnp.bfloat16))
    return jnp.concatenate(mixed, axis=1)


def solution(mesh):
    placed = (
        P(("groups", "expert"), "mp"),
        P(("groups", "expert"), None),
        P(("groups", "expert"), None),
        P(("groups", "expert"), None),
        P("expert", None, None, "mp"),
        P("expert", "mp", None),
    )
    return jax.shard_map(
        on_device,
        mesh=mesh,
        in_specs=placed,
        out_specs=P(("groups", "expert"), "mp"),
        check_vma=False,
    )
```

time: 219 us -> 145 us (0.66)
  local copies, waits for them, and re-layouts: 101 us -> 2.92 us
  Pallas kernels: 0 us -> 42.8 us
  matrix products: 40 us -> 2.12 us
  blocking collectives: 2.66 us -> 22.1 us
  waiting for transfers between devices: 42.6 us -> 53.4 us
  starting transfers between devices: 13 us -> 5.42 us
    dot_general x1 -> x0, local copies, waits for them, and re-layouts: 64.7 us -> none  [on_device(): jnp.dot(flat_rows, w_in[0].reshape(D, 2 * hid_local), preferred_element_t...]
    pallas_call x0 -> x3, Pallas kernels: none -> 42.8 us  [the longest x1 27.7 us: gate_up(): pl.pallas_call(functools.partial(gate_up_body, steps, first, last), grid=...]
    dot_general x5 -> x2, matrix products: 39.7 us -> 1.8 us  [the longest x1 1.2 us: on_device(): jnp.dot(combine, returned.astype(jnp.float32), preferred_element_type=jnp...]
    unnamed x6 -> x9, local copies, waits for them, and re-layouts: 35.5 us -> 2.49 us
    all_gather x0 -> x1, waiting for transfers between devices: none -> 23.3 us  [on_device(): rows = lax.all_gather(arrived, ('expert', 'mp'), axis_index_groups=pairs)]
    all_to_all x0 -> x1, blocking collectives: none -> 22.1 us  [on_device(): lax.all_to_all(outgoing, 'expert', split_axis=0, concat_axis=0, axis_inde...]
    ppermute x0 -> x2, waiting for transfers between devices: none -> 15.2 us  [the longest x1 15.2 us: on_device(): total = total + lax.ppermute(sent, 'expert', ring).astype(jnp.float32)]
    reduce_scatter x1 -> x0, waiting for transfers between devices: 14.1 us -> none  [on_device(): lax.psum_scatter(partial_value, 'mp', scatter_dimension=2, tiled=True)]
  transfers between devices with their start and end apart: 3 -> 4, of which waited for: 2 -> 3; matrix products, arithmetic and copies ran while one was open for 45% -> 0% of each run, Pallas kernels for 0% -> 5%
where the time goes in v1:
time: 145 us
  waiting for transfers between devices  53.4 us (37%)
  Pallas kernels  42.8 us (30%)
  blocking collectives  22.1 us (15%)
  between operations  13.5 us (9%)
  starting transfers between devices  5.42 us (4%)
  local copies, waits for them, and re-layouts  2.92 us (2%)
  other arithmetic  2.41 us (2%)
  matrix products  2.12 us (1%)
    pallas_call x1, Pallas kernels, gate_up(): pl.pallas_call(functools.partial(gate_up_body, steps, first, last), grid=...  27.7 us
    all_gather x1, waiting for transfers between devices, on_device(): rows = lax.all_gather(arrived, ('expert', 'mp'), axis_index_groups=pairs)  23.3 us
    all_to_all x1, blocking collectives, on_device(): lax.all_to_all(outgoing, 'expert', split_axis=0, concat_axis=0, axis_inde...  22.1 us
    ppermute x1, waiting for transfers between devices, on_device(): total = total + lax.ppermute(sent, 'expert', ring).astype(jnp.float32)  15.2 us
    pallas_call x2, Pallas kernels, down(): pl.pallas_call(down_body, grid_spec=pltpu.PrefetchScalarGridSpec(num_scal...  15.1 us
    all_to_all x1, waiting for transfers between devices, on_device(): lax.all_to_all(total, 'expert', split_axis=0, concat_axis=0, axis_index_g...  14.9 us
    all_to_all x1, starting transfers between devices, on_device(): lax.all_to_all(total, 'expert', split_axis=0, concat_axis=0, axis_index_g...  4.73 us
  transfers between devices with their start and end apart: 4, of which 3 were waited for; matrix products, arithmetic and copies ran while one was open for 0% of the time, Pallas kernels for 5%

profile of v1, /device:TPU:0, one launch (start us, length us, event | category | flops | bytes accessed | tf_op | source)
XLA Modules:
  0.0 144.8 jit_solution(4500948402517879423)
XLA Ops:
  6.5 0.8 copy.13
  7.4 0.1 reshape.64
  7.5 0.1 fusion.3
  7.6 0.2 reduce_window_sum.11
  7.8 0.8 select_reduce_fusion
  8.6 0.6 convolution_convert_fusion
  9.2 22.1 %all_to_all.10 = bf16[4,24,3072]{2,1,0:T(8,128)(2,1)} all-to-all(bf16[4,24,3072]{2,1,0:T(8,128)(2,1)S(1)} %bitcast.31), channel_id=1, replica_groups={{0,4,8,12},{2,6,10,14},{1,5,9,13},{3,7,11,15},{16,20,24,28},{18,22,26,3..., dimensions={0} | all-to-all | bytes 1179648 | tf_op jit(solution)/shard_map/all_to_all | solution.py:138
  31.4 0.0 all-gather.2.cloned.1.call-update
  31.4 23.3 %all-gather.2.cloned.1.call-done = bf16[4,96,3072]{2,1,0:T(8,128)(2,1)} async-done(((bf16[1,96,3072]{2,1,0:T(8,128)(2,1)}), bf16[4,96,3072]{2,1,0:T(8,128)(2,1)}) %all-gather.2.cloned.1.call-update) | async-done | bytes 2359312 | tf_op jit(solution)/shard_map/all_gather | solution.py:142
  54.7 1.7 %copy-done.2 = bf16[4,96,3072]{2,1,0:T(8,128)(2,1)S(1)} copy-done((bf16[4,96,3072]{2,1,0:T(8,128)(2,1)S(1)}, bf16[4,96,3072]{2,1,0:T(8,128)(2,1)}, u32[]{:S(2)}) %copy-start.2) | copy-done | bytes 2359320
  56.4 27.7 %shard_map.64.h_ref = bf16[192,2048]{1,0:T(8,128)(2,1)S(1)} custom-call(bf16[2,2,96,3072]{3,2,1,0:T(8,128)(2,1)S(1)} %bitcast.23, bf16[6144,32,128]{2,1,0:T(8,128)(2,1)} %bitcast.26), custom_call_target="tpu_custom_call" | custom-call | flops 9663676416 | bytes 50331648 | tf_op jit(solution)/shard_map/pallas_call | solution.py:62
  84.1 7.6 %shard_map.66 = bf16[192,3072]{1,0:T(8,128)(2,1)S(1)} custom-call(s32[1]{0:T(128)} %bitcast.9.at_ref, bf16[192,2048]{1,0:T(8,128)(2,1)S(1)} %shard_map.64.h_ref, bf16[2048,6144]{1,0:T(8,128)(2,1)} %bitcast.24), custom_call_target="tpu_custom_call" | custom-call | flops 2415919104 | bytes 12582912 | tf_op jit(solution)/shard_map/pallas_call | solution.py:80
  91.7 0.3 collective-permute-start
  92.0 7.6 %shard_map.65 = f32[192,3072]{1,0:T(8,128)S(1)} custom-call(s32[1]{0:T(128)} %bitcast.1.at_ref, bf16[192,2048]{1,0:T(8,128)(2,1)S(1)} %shard_map.64.h_ref, bf16[2048,6144]{1,0:T(8,128)(2,1)} %bitcast.25), custom_call_target="tpu_custom_call" | custom-call | flops 2415919104 | bytes 12582912 | tf_op jit(solution)/shard_map/pallas_call | solution.py:80
  99.6 0.3 add_convert_fusion
  99.9 0.4 collective-permute-start.1
  100.3 15.2 %collective-permute-done.1 = bf16[96,3072]{1,0:T(8,128)(2,1)S(1)} collective-permute-done((bf16[96,3072]{1,0:T(8,128)(2,1)S(1)}, bf16[96,3072]{1,0:T(8,128)(2,1)S(1)}, u32[]{:S(2)}, u32[]{:S(2)}) %collective-permute-start.1) | collective-permute-done | bytes 589856 | tf_op jit(solution)/shard_map/ppermute | solution.py:161
  115.5 1.0 fusion
  116.5 4.7 %all-to-all-start.1 = ((bf16[4,24,3072]{2,1,0:T(8,128)(2,1)}), bf16[4,24,3072]{2,1,0:T(8,128)(2,1)S(1)}, u32[]{:S(2)}, u32[]{:S(2)}) async-start(bf16[4,24,3072]{2,1,0:T(8,128)(2,1)} %bitcast.13), calls=%async_computation.1 | async-start | bytes 1179648 | tf_op jit(solution)/shard_map/all_to_all | solution.py:163
  121.2 0.1 copy.14
  121.3 0.1 mul.45
  121.5 0.3 fusion.1
  121.8 14.9 %all-to-all-done.1 = bf16[4,24,3072]{2,1,0:T(8,128)(2,1)S(1)} async-done(((bf16[4,24,3072]{2,1,0:T(8,128)(2,1)}), bf16[4,24,3072]{2,1,0:T(8,128)(2,1)S(1)}, u32[]{:S(2)}, u32[]{:S(2)}) %all-to-all-start.1) | async-done | bytes 589856 | tf_op jit(solution)/shard_map/all_to_all | solution.py:163
  136.7 1.2 convolution_convert_fusion.1
  (14 shorter events, 0.1 us)
Async XLA Ops:
  6.5 2.1 %copy-start = (bf16[64,3072]{1,0:T(8,128)(2,1)S(1)}, bf16[64,3072]{1,0:T(8,128)(2,1)}, u32[]{:S(2)}) copy-start(bf16[64,3072]{1,0:T(8,128)(2,1)} %param.6) | copy-start | bytes 1179652
  6.5 48.2 %all-gather.2.cloned.1.call-start = ((), (), s32[]{:S(2)}) async-start(), calls=%async_computation.2 | async-start | bytes 2949120 | tf_op jit(solution)/shard_map/all_gather | solution.py:142
  54.7 1.7 %copy-start.2 = (bf16[4,96,3072]{2,1,0:T(8,128)(2,1)S(1)}, bf16[4,96,3072]{2,1,0:T(8,128)(2,1)}, u32[]{:S(2)}) copy-start(bf16[4,96,3072]{2,1,0:T(8,128)(2,1)} %all-gather.2.cloned.1.call-done) | copy-start | bytes 7077892
  91.7 7.9 %collective-permute-start = (bf16[192,3072]{1,0:T(8,128)(2,1)S(1)}, bf16[192,3072]{1,0:T(8,128)(2,1)S(1)}, u32[]{:S(2)}, u32[]{:S(2)}) collective-permute-start(bf16[192,3072]{1,0:T(8,128)(2,1)S(1)} %shard_map.66), channel_id=1, source_target_pairs={{0,1},{1,0},{2,3},{3,2},{4,5},{5,4},{6,7},{7,6},{8,9},{9,8},{10,11... | collective-permute-start | bytes 3538952 | tf_op jit(solution)/shard_map/ppermute | solution.py:152
  99.9 15.6 %collective-permute-start.1 = (bf16[96,3072]{1,0:T(8,128)(2,1)S(1)}, bf16[96,3072]{1,0:T(8,128)(2,1)S(1)}, u32[]{:S(2)}, u32[]{:S(2)}) collective-permute-start(bf16[96,3072]{1,0:T(8,128)(2,1)S(1)} %dynamic-slice_bitcast_fusion), channel_id=1, source_target_pairs={{0,2},{2,0},{4,6},{6,4},{8,10},{10,8},{12,14},{14,12},{1,3},{3,1},... | collective-permute-start | bytes 1769480 | tf_op jit(solution)/shard_map/ppermute | solution.py:161
  100.3 20.9 %copy-start.3 = (s32[64,2]{0,1:T(2,128)S(1)}, s32[64,2]{0,1:T(2,128)}, u32[]{:S(2)}) copy-start(s32[64,2]{0,1:T(2,128)} %param.8) | copy-start | bytes 1540
  116.5 21.4 %copy-start.1 = (bf16[64,3072]{1,0:T(8,128)(2,1)S(1)}, bf16[64,3072]{1,0:T(8,128)(2,1)}, u32[]{:S(2)}) copy-start(bf16[64,3072]{1,0:T(8,128)(2,1)} %param.6) | copy-start | bytes 1179652
  116.5 20.2 %all-to-all-start.1 = ((bf16[4,24,3072]{2,1,0:T(8,128)(2,1)}), bf16[4,24,3072]{2,1,0:T(8,128)(2,1)S(1)}, u32[]{:S(2)}, u32[]{:S(2)}) async-start(bf16[4,24,3072]{2,1,0:T(8,128)(2,1)} %bitcast.13), calls=%async_computation.1 | async-start | bytes 1179648 | tf_op jit(solution)/shard_map/all_to_all | solution.py:163
Sparse Core Ops, SparseCore 0:
  31.5 23.1 all-gather.1

commit v2 on v1

--- a/solution.py
+++ b/solution.py
@@ -11,16 +11,16 @@
 EXP_WIN = 4
 CAP = 24
 
-CHUNKS = 1
+CHUNKS = 3
 STEP = 512
 COLS = 512
 
 
 def gate_up_body(steps, first, last, *refs):
     if first:
-        x_ref, w_ref, o_ref, *rest = refs
+        _, own_ref, other_ref, w_ref, o_ref, *rest = refs
     else:
-        x_ref, w_ref, before_ref, o_ref, *rest = refs
+        _, own_ref, other_ref, w_ref, before_ref, o_ref, *rest = refs
     sums = rest[0] if last else o_ref
     step = pl.program_id(0)
 
@@ -29,8 +29,7 @@
         sums[...] = jnp.zeros_like(sums) if first else before_ref[...]
 
     depth = w_ref.shape[0]
-    rows = x_ref.shape[0] * x_ref.shape[1]
-    x = x_ref[...].reshape(rows, depth)
+    x = jnp.where(step < steps // 2, own_ref[...], other_ref[...])
     w = w_ref[...].reshape(depth, sums.shape[1])
     sums[...] += jnp.dot(x, w, preferred_element_type=jnp.float32)
 
@@ -43,32 +42,33 @@
                 o_ref[:, 128 * j:128 * j + 128] = (gate * jax.nn.sigmoid(gate) * up).astype(o_ref.dtype)
 
 
-def gate_up(x, w, before, chunk, last):
-    ranks, halves, depth, width = x.shape
-    rows = ranks * depth
+def gate_up(own, other, w, before, at, last):
+    rows, width = own.shape
     wide = w.shape[1] * 128
     per_half = width // STEP
-    half = w.shape[0] // halves // STEP
-    steps = halves * per_half
+    steps = 2 * per_half
     first = before is None
     in_specs = [
-        pl.BlockSpec((ranks, None, depth, STEP), lambda k: (0, k // per_half, 0, k % per_half)),
-        pl.BlockSpec((STEP, w.shape[1], 128),
-                     lambda k: (k // per_half * half + chunk * per_half + k % per_half, 0, 0)),
+        pl.BlockSpec((rows, STEP), lambda k, at: (0, jnp.minimum(k, per_half - 1))),
+        pl.BlockSpec((rows, STEP), lambda k, at: (0, jnp.maximum(k - per_half, 0))),
+        pl.BlockSpec((STEP, w.shape[1], 128), lambda k, at: (at[k // per_half] + k % per_half, 0, 0)),
     ]
     if not first:
-        in_specs.append(pl.BlockSpec((rows, wide), lambda k: (0, 0)))
+        in_specs.append(pl.BlockSpec((rows, wide), lambda k, at: (0, 0)))
     out = jax.ShapeDtypeStruct((rows, wide // 2), jnp.bfloat16) if last else jax.ShapeDtypeStruct((rows, wide), jnp.float32)
     return pl.pallas_call(
         functools.partial(gate_up_body, steps, first, last),
-        grid=(steps,),
-        in_specs=in_specs,
-        out_specs=pl.BlockSpec(out.shape, lambda k: (0, 0)),
+        grid_spec=pltpu.PrefetchScalarGridSpec(
+            num_scalar_prefetch=1,
+            grid=(steps,),
+            in_specs=in_specs,
+            out_specs=pl.BlockSpec(out.shape, lambda k, at: (0, 0)),
+            scratch_shapes=[pltpu.VMEM((rows, wide), jnp.float32)] if last else [],
+        ),
         out_shape=out,
-        scratch_shapes=[pltpu.VMEM((rows, wide), jnp.float32)] if last else [],
         compiler_params=pltpu.CompilerParams(vmem_limit_bytes=48 * 2**20),
-        cost_estimate=pl.CostEstimate(flops=2 * rows * halves * width * wide, bytes_accessed=halves * width * wide * 2, transcendentals=0),
-    )(*([x, w] if first else [x, w, before]))
+        cost_estimate=pl.CostEstimate(flops=4 * rows * width * wide, bytes_accessed=4 * width * wide, transcendentals=0),
+    )(*([at, own, other, w] if first else [at, own, other, w, before]))
 
 
 def down_body(at_ref, h_ref, w_ref, o_ref):
@@ -108,7 +108,8 @@
     keep_mask = (chosen < EXP_WIN) & (position < limit_of)
     rank_vals = gate_ranks.astype(jnp.float32)
     gate_share = (rank_vals / jnp.sum(rank_vals, axis=1, keepdims=True)).reshape(-1)
-    slot_index = chosen * CAP + position
+    turned = lax.rem(chosen - lax.axis_index("expert") // slices + NUM_EXPERTS, EXP_WIN)
+    slot_index = turned * CAP + position
     columns = jnp.arange(EXP_WIN * CAP, dtype=jnp.int32)
     select = (keep_mask[:, None] & (slot_index[:, None] == columns[None, :])).astype(jnp.float32)
     owners = (
@@ -124,24 +125,30 @@
     )
     half = tokens.shape[1]
     width = half // CHUNKS
-    same_rank = [[e * slices + r for e in range(EXP_WIN)] for r in range(slices)]
-    same_expert = [[e * slices + r for r in range(slices)] for e in range(EXP_WIN)]
     core = lax.axis_index("mp")
+    spots = [(e, r) for e in range(EXP_WIN) for r in range(slices)]
+
+    def to_expert(x, d):
+        return lax.ppermute(x, "expert", [(e * slices + r, (e + d) % EXP_WIN * slices + r) for e, r in spots])
+
+    def to_rank(x, d):
+        return lax.ppermute(x, "expert", [(e * slices + r, e * slices + (r + d) % slices) for e, r in spots])
+
+    def to_core(x):
+        return lax.ppermute(x, "mp", [(0, 1), (1, 0)])
+
     weights = w_in[0].reshape(D, 2, hid_local // 128, 128).transpose(0, 2, 1, 3)
     weights = weights.reshape(D, hid_local // 64, 128)
+    outgoing = jnp.dot(pick_matrix, tokens, preferred_element_type=jnp.float32).astype(jnp.bfloat16)
 
     sums = None
     for c in range(CHUNKS):
-        part = tokens[:, c * width:(c + 1) * width]
-        outgoing = jnp.dot(pick_matrix, part, preferred_element_type=jnp.float32).astype(jnp.bfloat16)
-        outgoing = outgoing.reshape(EXP_WIN, CAP, width)
-        arrived = lax.all_to_all(
-            outgoing, "expert", split_axis=0, concat_axis=0, axis_index_groups=same_rank, tiled=True
-        ).reshape(EXP_WIN * CAP, width)
-        pairs = [[2 * i + m for i in group for m in range(2)] for group in same_expert]
-        rows = lax.all_gather(arrived, ("expert", "mp"), axis_index_groups=pairs)
-        rows = rows.reshape(slices, 2, EXP_WIN * CAP, width)
-        sums = gate_up(rows, weights, sums, c, c == CHUNKS - 1)
+        part = outgoing[:, c * width:(c + 1) * width].reshape(EXP_WIN, CAP, width)
+        arrived = jnp.concatenate([part[0]] + [to_expert(part[d], d) for d in range(1, EXP_WIN)], axis=0)
+        own = jnp.concatenate([arrived] + [to_rank(arrived, d) for d in range(1, slices)], axis=0)
+        other = to_core(own)
+        at = (jnp.stack([core, 1 - core]) * half + c * width) // STEP
+        sums = gate_up(own, other, weights, sums, at.astype(jnp.int32), c == CHUNKS - 1)
     hidden = sums
 
     mixed = []
@@ -149,20 +156,15 @@
         tiles = half // COLS
         start = c * (width // COLS)
         theirs = down(hidden, w_out[0], (1 - core) * tiles + start, width, jnp.bfloat16)
-        landed = lax.ppermute(theirs, "mp", [(0, 1), (1, 0)])
+        landed = to_core(theirs)
         mine = down(hidden, w_out[0], core * tiles + start, width, jnp.float32)
         share = (mine + landed.astype(jnp.float32)).astype(jnp.bfloat16)
         share = share.reshape(slices, EXP_WIN * CAP, width)
-        rank = lax.rem(lax.axis_index("expert"), slices)
-        total = lax.dynamic_index_in_dim(share, rank, 0, False).astype(jnp.float32)
+        total = share[0].astype(jnp.float32)
         for d in range(1, slices):
-            sent = lax.dynamic_index_in_dim(share, lax.rem(rank + d, slices), 0, False)
-            ring = [(g[r], g[(r + d) % slices]) for g in same_expert for r in range(slices)]
-            total = total + lax.ppermute(sent, "expert", ring).astype(jnp.float32)
+            total = total + to_rank(share[d], slices - d).astype(jnp.float32)
         total = total.astype(jnp.bfloat16).reshape(EXP_WIN, CAP, width)
-        returned = lax.all_to_all(
-            total, "expert", split_axis=0, concat_axis=0, axis_index_groups=same_rank, tiled=True
-        ).reshape(EXP_WIN * CAP, width)
+        returned = jnp.concatenate([total[0]] + [to_expert(total[d], EXP_WIN - d) for d in range(1, EXP_WIN)], axis=0)
         mixed.append(jnp.dot(
             combine,
             returned.astype(jnp.float32),

time: 145 us -> 118 us (0.81)
  waiting for transfers between devices: 53.4 us -> 20.2 us
  starting transfers between devices: 5.42 us -> 35 us
  blocking collectives: 22.1 us -> 0 us
  between operations: 13.5 us -> 0.49 us
  Pallas kernels: 42.8 us -> 53.1 us
    ppermute x2 -> x30, starting transfers between devices: 0.69 us -> 35 us  [the longest x18 26.2 us: to_expert(): lax.ppermute(x, 'expert', [(e * slices + r, (e + d) % EXP_WIN * slices +...]
    all_gather x1 -> x0, waiting for transfers between devices: 23.3 us -> none  [on_device(): rows = lax.all_gather(arrived, ('expert', 'mp'), axis_index_groups=pairs)]
    all_to_all x1 -> x0, blocking collectives: 22.1 us -> none  [on_device(): lax.all_to_all(outgoing, 'expert', split_axis=0, concat_axis=0, axis_inde...]
    all_to_all x1 -> x0, waiting for transfers between devices: 14.9 us -> none  [on_device(): lax.all_to_all(total, 'expert', split_axis=0, concat_axis=0, axis_index_g...]
    pallas_call x1 -> x3, Pallas kernels: 27.7 us -> 35.9 us  [gate_up(): pl.pallas_call(functools.partial(gate_up_body, steps, first, last), grid_...]
    ppermute x2 -> x30, waiting for transfers between devices: 15.2 us -> 20.2 us  [the longest x6 15.1 us: to_rank(): lax.ppermute(x, 'expert', [(e * slices + r, e * slices + (r + d) % slices...]
    all_to_all x1 -> x0, starting transfers between devices: 4.73 us -> none  [on_device(): lax.all_to_all(total, 'expert', split_axis=0, concat_axis=0, axis_index_g...]
    pallas_call x2 -> x6, Pallas kernels: 15.1 us -> 17.2 us  [down(): pl.pallas_call(down_body, grid_spec=pltpu.PrefetchScalarGridSpec(num_scal...]
  transfers between devices with their start and end apart: 4 -> 30, of which waited for: 3 -> 10; matrix products, arithmetic and copies ran while one was open for 0% -> 3% of each run, Pallas kernels for 5% -> 33%
where the time goes in v2:
time: 118 us; the launch traced here: 117 us
  Pallas kernels  53.1 us (45%)
  starting transfers between devices  35 us (30%)
  waiting for transfers between devices  20.2 us (17%)
  other arithmetic  3.84 us (3%)
  local copies, waits for them, and re-layouts  3.08 us (3%)
  matrix products  1.63 us (1%)
    pallas_call x3, Pallas kernels, gate_up(): pl.pallas_call(functools.partial(gate_up_body, steps, first, last), grid_...  35.9 us
    ppermute x18, starting transfers between devices, to_expert(): lax.ppermute(x, 'expert', [(e * slices + r, (e + d) % EXP_WIN * slices +...  26.2 us
    pallas_call x6, Pallas kernels, down(): pl.pallas_call(down_body, grid_spec=pltpu.PrefetchScalarGridSpec(num_scal...  17.2 us
    ppermute x6, waiting for transfers between devices, to_rank(): lax.ppermute(x, 'expert', [(e * slices + r, e * slices + (r + d) % slices...  15.1 us
    ppermute x6, starting transfers between devices, to_rank(): lax.ppermute(x, 'expert', [(e * slices + r, e * slices + (r + d) % slices...  7.37 us
    ppermute x18, waiting for transfers between devices, to_expert(): lax.ppermute(x, 'expert', [(e * slices + r, (e + d) % EXP_WIN * slices +...  5.03 us
    unnamed x16, local copies, waits for them, and re-layouts  2.5 us
  transfers between devices with their start and end apart: 30, of which 10 were waited for; matrix products, arithmetic and copies ran while one was open for 3% of the time, Pallas kernels for 33%

profile of v2, /device:TPU:0, one launch (start us, length us, event | category | flops | bytes accessed | tf_op | source)
XLA Modules:
  0.0 117.2 jit_solution(11017569024910448673)
XLA Ops:
  2.7 3.1 %collective-permute-start.10 = (bf16[24,1024]{1,0:T(8,128)(2,1)S(1)}, bf16[24,1024]{1,0:T(8,128)(2,1)S(1)}, u32[]{:S(2)}, u32[]{:S(2)}) collective-permute-start(bf16[24,1024]{1,0:T(8,128)(2,1)S(1)} %get-tuple-element.15), channel_id=1, source_target_pairs={{0,4},{2,6},{4,8},{6,10},{8,12},{10,14},{12,0},{14,2},{1,5},{3,7},... | collective-permute-start | bytes 147464 | tf_op jit(solution)/shard_map/ppermute | solution.py:132
  5.8 2.6 %collective-permute-start.11 = (bf16[24,1024]{1,0:T(8,128)(2,1)S(1)}, bf16[24,1024]{1,0:T(8,128)(2,1)S(1)}, u32[]{:S(2)}, u32[]{:S(2)}) collective-permute-start(bf16[24,1024]{1,0:T(8,128)(2,1)S(1)} %get-tuple-element.14), channel_id=1, source_target_pairs={{0,8},{2,10},{4,12},{6,14},{8,0},{10,2},{12,4},{14,6},{1,9},{3,11}... | collective-permute-start | bytes 147464 | tf_op jit(solution)/shard_map/ppermute | solution.py:132
  12.5 2.9 %collective-permute-start.7 = (bf16[24,1024]{1,0:T(8,128)(2,1)S(1)}, bf16[24,1024]{1,0:T(8,128)(2,1)S(1)}, u32[]{:S(2)}, u32[]{:S(2)}) collective-permute-start(bf16[24,1024]{1,0:T(8,128)(2,1)S(1)} %get-tuple-element.16), channel_id=1, source_target_pairs={{0,12},{2,14},{4,0},{6,2},{8,4},{10,6},{12,8},{14,10},{1,13},{3,15... | collective-permute-start | bytes 147464 | tf_op jit(solution)/shard_map/ppermute | solution.py:132
  17.5 2.9 %collective-permute-start.2 = (bf16[24,1024]{1,0:T(8,128)(2,1)S(1)}, bf16[24,1024]{1,0:T(8,128)(2,1)S(1)}, u32[]{:S(2)}, u32[]{:S(2)}) collective-permute-start(bf16[24,1024]{1,0:T(8,128)(2,1)S(1)} %get-tuple-element.20), channel_id=1, source_target_pairs={{0,12},{2,14},{4,0},{6,2},{8,4},{10,6},{12,8},{14,10},{1,13},{3,15... | collective-permute-start | bytes 147464 | tf_op jit(solution)/shard_map/ppermute | solution.py:132
  24.2 4.1 %collective-permute-done.13 = bf16[96,1024]{1,0:T(8,128)(2,1)S(1)} collective-permute-done((bf16[96,1024]{1,0:T(8,128)(2,1)S(1)}, bf16[96,1024]{1,0:T(8,128)(2,1)S(1)}, u32[]{:S(2)}, u32[]{:S(2)}) %collective-permute-start.13) | collective-permute-done | bytes 196640 | tf_op jit(solution)/shard_map/ppermute | solution.py:135
  28.4 2.5 %collective-permute-done.8 = bf16[96,1024]{1,0:T(8,128)(2,1)S(1)} collective-permute-done((bf16[96,1024]{1,0:T(8,128)(2,1)S(1)}, bf16[96,1024]{1,0:T(8,128)(2,1)S(1)}, u32[]{:S(2)}, u32[]{:S(2)}) %collective-permute-start.8) | collective-permute-done | bytes 196640 | tf_op jit(solution)/shard_map/ppermute | solution.py:135
  31.0 2.0 %collective-permute-done.3 = bf16[96,1024]{1,0:T(8,128)(2,1)S(1)} collective-permute-done((bf16[96,1024]{1,0:T(8,128)(2,1)S(1)}, bf16[96,1024]{1,0:T(8,128)(2,1)S(1)}, u32[]{:S(2)}, u32[]{:S(2)}) %collective-permute-start.3) | collective-permute-done | bytes 196640 | tf_op jit(solution)/shard_map/ppermute | solution.py:135
  33.1 11.6 %shard_map.64.refs_4_ = f32[192,4096]{1,0:T(8,128)S(1)} custom-call(s32[2]{0:T(128)S(1)} %get-tuple-element.7.refs_0_, bf16[192,1024]{1,0:T(8,128)(2,1)S(1)} %constant_dynamic-update-slice_fusion.10.refs_1_, bf16[192,1024]{1,0:T(8,128)(2,1)S(1)} %collective-permute-done.14.refs_2_, bf16[6144,32,128]{2,1,0:T(8,128)(2,1)} %bitcast.25), custom_call_target="tpu_custom_call" | custom-call | flops 3221225472 | bytes 16777216 | tf_op jit(solution)/shard_map/pallas_call | solution.py:59
  44.7 1.6 %copy-done.2 = f32[192,4096]{1,0:T(8,128)} copy-done((f32[192,4096]{1,0:T(8,128)}, f32[192,4096]{1,0:T(8,128)S(1)}, u32[]{:S(2)}) %copy-start.2) | copy-done | bytes 3145752
  46.3 12.6 %shard_map.65.refs_4_ = f32[192,4096]{1,0:T(8,128)S(1)} custom-call(s32[2]{0:T(128)S(1)} %get-tuple-element.36.refs_0_, bf16[192,1024]{1,0:T(8,128)(2,1)S(1)} %constant_dynamic-update-slice_fusion.5.refs_1_, bf16[192,1024]{1,0:T(8,128)(2,1)S(1)} %collective-permute-done.9.refs_2_, bf16[6144,32,128]{2,1,0:T(8,128)(2,1)} %bitcast.26, f32[192,4096]{1,0:T(8,128)} %copy-done.2), custom_call_target="tpu_custom_call" | custom-call | flops 3221225472 | bytes 16777216 | tf_op jit(solution)/shard_map/pallas_call | solution.py:59
  58.9 11.7 %shard_map.66.h_ref = bf16[192,2048]{1,0:T(8,128)(2,1)S(1)} custom-call(s32[2]{0:T(128)S(1)} %get-tuple-element.37.refs_0_, bf16[192,1024]{1,0:T(8,128)(2,1)S(1)} %constant_dynamic-update-slice_fusion.refs_1_, bf16[192,1024]{1,0:T(8,128)(2,1)S(1)} %collective-permute-done.4.refs_2_, bf16[6144,32,128]{2,1,0:T(8,128)(2,1)} %bitcast.27, ...), custom_call_target="tpu_custom_call" | custom-call | flops 3221225472 | bytes 16777216 | tf_op jit(solution)/shard_map/pallas_call | solution.py:59
  70.6 2.9 %shard_map.68 = bf16[192,1024]{1,0:T(8,128)(2,1)S(1)} custom-call(s32[1]{0:T(128)} %bitcast.10.at_ref, bf16[192,2048]{1,0:T(8,128)(2,1)S(1)} %shard_map.66.h_ref, bf16[2048,6144]{1,0:T(8,128)(2,1)} %bitcast.19), custom_call_target="tpu_custom_call" | custom-call | flops 805306368 | bytes 4194304 | tf_op jit(solution)/shard_map/pallas_call | solution.py:80
  74.4 2.9 %shard_map.70 = bf16[192,1024]{1,0:T(8,128)(2,1)S(1)} custom-call(s32[1]{0:T(128)} %bitcast.12.at_ref, bf16[192,2048]{1,0:T(8,128)(2,1)S(1)} %shard_map.66.h_ref, bf16[2048,6144]{1,0:T(8,128)(2,1)} %bitcast.20), custom_call_target="tpu_custom_call" | custom-call | flops 805306368 | bytes 4194304 | tf_op jit(solution)/shard_map/pallas_call | solution.py:80
  77.3 2.9 %shard_map.72 = bf16[192,1024]{1,0:T(8,128)(2,1)S(1)} custom-call(s32[1]{0:T(128)} %bitcast.14.at_ref, bf16[192,2048]{1,0:T(8,128)(2,1)S(1)} %shard_map.66.h_ref, bf16[2048,6144]{1,0:T(8,128)(2,1)} %bitcast.21), custom_call_target="tpu_custom_call" | custom-call | flops 805306368 | bytes 4194304 | tf_op jit(solution)/shard_map/pallas_call | solution.py:80
  80.7 2.9 %shard_map.67 = f32[192,1024]{1,0:T(8,128)S(1)} custom-call(s32[1]{0:T(128)} %bitcast.1.at_ref, bf16[192,2048]{1,0:T(8,128)(2,1)S(1)} %shard_map.66.h_ref, bf16[2048,6144]{1,0:T(8,128)(2,1)} %bitcast.22), custom_call_target="tpu_custom_call" | custom-call | flops 805306368 | bytes 4194304 | tf_op jit(solution)/shard_map/pallas_call | solution.py:80
  83.6 2.9 %shard_map.69 = f32[192,1024]{1,0:T(8,128)S(1)} custom-call(s32[1]{0:T(128)} %bitcast.11.at_ref, bf16[192,2048]{1,0:T(8,128)(2,1)S(1)} %shard_map.66.h_ref, bf16[2048,6144]{1,0:T(8,128)(2,1)} %bitcast.23), custom_call_target="tpu_custom_call" | custom-call | flops 805306368 | bytes 4194304 | tf_op jit(solution)/shard_map/pallas_call | solution.py:80
  86.5 2.9 %shard_map.71 = f32[192,1024]{1,0:T(8,128)S(1)} custom-call(s32[1]{0:T(128)} %bitcast.13.at_ref, bf16[192,2048]{1,0:T(8,128)(2,1)S(1)} %shard_map.66.h_ref, bf16[2048,6144]{1,0:T(8,128)(2,1)} %bitcast.24), custom_call_target="tpu_custom_call" | custom-call | flops 805306368 | bytes 4194304 | tf_op jit(solution)/shard_map/pallas_call | solution.py:80
  89.5 1.6 %collective-permute-start.16 = (bf16[96,1024]{1,0:T(8,128)(2,1)S(1)}, bf16[96,1024]{1,0:T(8,128)(2,1)S(1)}, u32[]{:S(2)}, u32[]{:S(2)}) collective-permute-start(bf16[96,1024]{1,0:T(8,128)(2,1)S(1)} %slice.178), channel_id=1, source_target_pairs={{0,2},{2,0},{4,6},{6,4},{8,10},{10,8},{12,14},{14,12},{1,3},{3,1},... | collective-permute-start | bytes 589832 | tf_op jit(solution)/shard_map/ppermute | solution.py:135
  91.9 1.6 %collective-permute-start.26 = (bf16[96,1024]{1,0:T(8,128)(2,1)S(1)}, bf16[96,1024]{1,0:T(8,128)(2,1)S(1)}, u32[]{:S(2)}, u32[]{:S(2)}) collective-permute-start(bf16[96,1024]{1,0:T(8,128)(2,1)S(1)} %slice.190), channel_id=1, source_target_pairs={{0,2},{2,0},{4,6},{6,4},{8,10},{10,8},{12,14},{14,12},{1,3},{3,1},... | collective-permute-start | bytes 589832 | tf_op jit(solution)/shard_map/ppermute | solution.py:135
  93.5 3.9 %collective-permute-done.16 = bf16[96,1024]{1,0:T(8,128)(2,1)S(1)} collective-permute-done((bf16[96,1024]{1,0:T(8,128)(2,1)S(1)}, bf16[96,1024]{1,0:T(8,128)(2,1)S(1)}, u32[]{:S(2)}, u32[]{:S(2)}) %collective-permute-start.16) | collective-permute-done | bytes 196640 | tf_op jit(solution)/shard_map/ppermute | solution.py:135
  99.0 1.7 %collective-permute-start.19 = (bf16[24,1024]{1,0:T(8,128)(2,1)S(1)}, bf16[24,1024]{1,0:T(8,128)(2,1)S(1)}, u32[]{:S(2)}, u32[]{:S(2)}) collective-permute-start(bf16[24,1024]{1,0:T(8,128)(2,1)S(1)} %get-tuple-element.25), channel_id=1, source_target_pairs={{0,4},{2,6},{4,8},{6,10},{8,12},{10,14},{12,0},{14,2},{1,5},{3,7},... | collective-permute-start | bytes 147464 | tf_op jit(solution)/shard_map/ppermute | solution.py:132
  103.0 1.9 %collective-permute-done.26 = bf16[96,1024]{1,0:T(8,128)(2,1)S(1)} collective-permute-done((bf16[96,1024]{1,0:T(8,128)(2,1)S(1)}, bf16[96,1024]{1,0:T(8,128)(2,1)S(1)}, u32[]{:S(2)}, u32[]{:S(2)}) %collective-permute-start.26) | collective-permute-done | bytes 196640 | tf_op jit(solution)/shard_map/ppermute | solution.py:135
  106.2 3.8 %collective-permute-start.27 = (bf16[24,1024]{1,0:T(8,128)(2,1)S(1)}, bf16[24,1024]{1,0:T(8,128)(2,1)S(1)}, u32[]{:S(2)}, u32[]{:S(2)}) collective-permute-start(bf16[24,1024]{1,0:T(8,128)(2,1)S(1)} %get-tuple-element.35), channel_id=1, source_target_pairs={{0,12},{2,14},{4,0},{6,2},{8,4},{10,6},{12,8},{14,10},{1,13},{3,15... | collective-permute-start | bytes 147464 | tf_op jit(solution)/shard_map/ppermute | solution.py:132
  112.3 2.6 %collective-permute-done.28 = bf16[24,1024]{1,0:T(8,128)(2,1)S(1)} collective-permute-done((bf16[24,1024]{1,0:T(8,128)(2,1)S(1)}, bf16[24,1024]{1,0:T(8,128)(2,1)S(1)}, u32[]{:S(2)}, u32[]{:S(2)}) %collective-permute-start.28) | collective-permute-done | bytes 49184 | tf_op jit(solution)/shard_map/ppermute | solution.py:132
  (98 shorter events, 25.2 us)
Async XLA Ops:
  2.7 9.8 %collective-permute-start.10 = (bf16[24,1024]{1,0:T(8,128)(2,1)S(1)}, bf16[24,1024]{1,0:T(8,128)(2,1)S(1)}, u32[]{:S(2)}, u32[]{:S(2)}) collective-permute-start(bf16[24,1024]{1,0:T(8,128)(2,1)S(1)} %get-tuple-element.15), channel_id=1, source_target_pairs={{0,4},{2,6},{4,8},{6,10},{8,12},{10,14},{12,0},{14,2},{1,5},{3,7},... | collective-permute-start | bytes 147464 | tf_op jit(solution)/shard_map/ppermute | solution.py:132
  5.8 9.6 %collective-permute-start.11 = (bf16[24,1024]{1,0:T(8,128)(2,1)S(1)}, bf16[24,1024]{1,0:T(8,128)(2,1)S(1)}, u32[]{:S(2)}, u32[]{:S(2)}) collective-permute-start(bf16[24,1024]{1,0:T(8,128)(2,1)S(1)} %get-tuple-element.14), channel_id=1, source_target_pairs={{0,8},{2,10},{4,12},{6,14},{8,0},{10,2},{12,4},{14,6},{1,9},{3,11}... | collective-permute-start | bytes 147464 | tf_op jit(solution)/shard_map/ppermute | solution.py:132
  8.4 7.6 %collective-permute-start.12 = (bf16[24,1024]{1,0:T(8,128)(2,1)S(1)}, bf16[24,1024]{1,0:T(8,128)(2,1)S(1)}, u32[]{:S(2)}, u32[]{:S(2)}) collective-permute-start(bf16[24,1024]{1,0:T(8,128)(2,1)S(1)} %get-tuple-element.13), channel_id=1, source_target_pairs={{0,12},{2,14},{4,0},{6,2},{8,4},{10,6},{12,8},{14,10},{1,13},{3,15... | collective-permute-start | bytes 147464 | tf_op jit(solution)/shard_map/ppermute | solution.py:132
  9.8 7.7 %collective-permute-start.5 = (bf16[24,1024]{1,0:T(8,128)(2,1)S(1)}, bf16[24,1024]{1,0:T(8,128)(2,1)S(1)}, u32[]{:S(2)}, u32[]{:S(2)}) collective-permute-start(bf16[24,1024]{1,0:T(8,128)(2,1)S(1)} %get-tuple-element.18), channel_id=1, source_target_pairs={{0,4},{2,6},{4,8},{6,10},{8,12},{10,14},{12,0},{14,2},{1,5},{3,7},... | collective-permute-start | bytes 147464 | tf_op jit(solution)/shard_map/ppermute | solution.py:132
  10.4 10.0 %collective-permute-start.6 = (bf16[24,1024]{1,0:T(8,128)(2,1)S(1)}, bf16[24,1024]{1,0:T(8,128)(2,1)S(1)}, u32[]{:S(2)}, u32[]{:S(2)}) collective-permute-start(bf16[24,1024]{1,0:T(8,128)(2,1)S(1)} %get-tuple-element.17), channel_id=1, source_target_pairs={{0,8},{2,10},{4,12},{6,14},{8,0},{10,2},{12,4},{14,6},{1,9},{3,11}... | collective-permute-start | bytes 147464 | tf_op jit(solution)/shard_map/ppermute | solution.py:132
  12.5 9.4 %collective-permute-start.7 = (bf16[24,1024]{1,0:T(8,128)(2,1)S(1)}, bf16[24,1024]{1,0:T(8,128)(2,1)S(1)}, u32[]{:S(2)}, u32[]{:S(2)}) collective-permute-start(bf16[24,1024]{1,0:T(8,128)(2,1)S(1)} %get-tuple-element.16), channel_id=1, source_target_pairs={{0,12},{2,14},{4,0},{6,2},{8,4},{10,6},{12,8},{14,10},{1,13},{3,15... | collective-permute-start | bytes 147464 | tf_op jit(solution)/shard_map/ppermute | solution.py:132
  15.4 7.2 %collective-permute-start = (bf16[24,1024]{1,0:T(8,128)(2,1)S(1)}, bf16[24,1024]{1,0:T(8,128)(2,1)S(1)}, u32[]{:S(2)}, u32[]{:S(2)}) collective-permute-start(bf16[24,1024]{1,0:T(8,128)(2,1)S(1)} %get-tuple-element.22), channel_id=1, source_target_pairs={{0,4},{2,6},{4,8},{6,10},{8,12},{10,14},{12,0},{14,2},{1,5},{3,7},... | collective-permute-start | bytes 147464 | tf_op jit(solution)/shard_map/ppermute | solution.py:132
  16.0 6.5 %collective-permute-start.1 = (bf16[24,1024]{1,0:T(8,128)(2,1)S(1)}, bf16[24,1024]{1,0:T(8,128)(2,1)S(1)}, u32[]{:S(2)}, u32[]{:S(2)}) collective-permute-start(bf16[24,1024]{1,0:T(8,128)(2,1)S(1)} %get-tuple-element.21), channel_id=1, source_target_pairs={{0,8},{2,10},{4,12},{6,14},{8,0},{10,2},{12,4},{14,6},{1,9},{3,11}... | collective-permute-start | bytes 147464 | tf_op jit(solution)/shard_map/ppermute | solution.py:132
  20.4 7.8 %collective-permute-start.13 = (bf16[96,1024]{1,0:T(8,128)(2,1)S(1)}, bf16[96,1024]{1,0:T(8,128)(2,1)S(1)}, u32[]{:S(2)}, u32[]{:S(2)}) collective-permute-start(bf16[96,1024]{1,0:T(8,128)(2,1)S(1)} %pad_maximum_fusion.3), channel_id=1, source_target_pairs={{0,2},{2,0},{4,6},{6,4},{8,10},{10,8},{12,14},{14,12},{1,3},{3,1},... | collective-permute-start | bytes 589832 | tf_op jit(solution)/shard_map/ppermute | solution.py:135
  21.9 8.9 %collective-permute-start.8 = (bf16[96,1024]{1,0:T(8,128)(2,1)S(1)}, bf16[96,1024]{1,0:T(8,128)(2,1)S(1)}, u32[]{:S(2)}, u32[]{:S(2)}) collective-permute-start(bf16[96,1024]{1,0:T(8,128)(2,1)S(1)} %pad_maximum_fusion.2), channel_id=1, source_target_pairs={{0,2},{2,0},{4,6},{6,4},{8,10},{10,8},{12,14},{14,12},{1,3},{3,1},... | collective-permute-start | bytes 589832 | tf_op jit(solution)/shard_map/ppermute | solution.py:135
  22.6 10.4 %collective-permute-start.3 = (bf16[96,1024]{1,0:T(8,128)(2,1)S(1)}, bf16[96,1024]{1,0:T(8,128)(2,1)S(1)}, u32[]{:S(2)}, u32[]{:S(2)}) collective-permute-start(bf16[96,1024]{1,0:T(8,128)(2,1)S(1)} %pad_maximum_fusion.1), channel_id=1, source_target_pairs={{0,2},{2,0},{4,6},{6,4},{8,10},{10,8},{12,14},{14,12},{1,3},{3,1},... | collective-permute-start | bytes 589832 | tf_op jit(solution)/shard_map/ppermute | solution.py:135
  30.9 15.4 %collective-permute-start.9 = (bf16[192,1024]{1,0:T(8,128)(2,1)S(1)}, bf16[192,1024]{1,0:T(8,128)(2,1)S(1)}, u32[]{:S(2)}, u32[]{:S(2)}) collective-permute-start(bf16[192,1024]{1,0:T(8,128)(2,1)S(1)} %constant_dynamic-update-slice_fusion.5.refs_1_), channel_id=1, source_target_pairs={{0,1},{1,0},{2,3},{3,2},{4,5},{5,4},{6,7},{7,6},{8,9},{9,8},{10,11... | collective-permute-start | bytes 1179656 | tf_op jit(solution)/shard_map/ppermute | solution.py:138
  33.0 25.9 %collective-permute-start.4 = (bf16[192,1024]{1,0:T(8,128)(2,1)S(1)}, bf16[192,1024]{1,0:T(8,128)(2,1)S(1)}, u32[]{:S(2)}, u32[]{:S(2)}) collective-permute-start(bf16[192,1024]{1,0:T(8,128)(2,1)S(1)} %constant_dynamic-update-slice_fusion.refs_1_), channel_id=1, source_target_pairs={{0,1},{1,0},{2,3},{3,2},{4,5},{5,4},{6,7},{7,6},{8,9},{9,8},{10,11... | collective-permute-start | bytes 1179656 | tf_op jit(solution)/shard_map/ppermute | solution.py:138
  73.5 15.9 %collective-permute-start.15 = (bf16[192,1024]{1,0:T(8,128)(2,1)S(1)}, bf16[192,1024]{1,0:T(8,128)(2,1)S(1)}, u32[]{:S(2)}, u32[]{:S(2)}) collective-permute-start(bf16[192,1024]{1,0:T(8,128)(2,1)S(1)} %shard_map.68), channel_id=1, source_target_pairs={{0,1},{1,0},{2,3},{3,2},{4,5},{5,4},{6,7},{7,6},{8,9},{9,8},{10,11... | collective-permute-start | bytes 1179656 | tf_op jit(solution)/shard_map/ppermute | solution.py:138
  77.2 13.8 %collective-permute-start.20 = (bf16[192,1024]{1,0:T(8,128)(2,1)S(1)}, bf16[192,1024]{1,0:T(8,128)(2,1)S(1)}, u32[]{:S(2)}, u32[]{:S(2)}) collective-permute-start(bf16[192,1024]{1,0:T(8,128)(2,1)S(1)} %shard_map.70), channel_id=1, source_target_pairs={{0,1},{1,0},{2,3},{3,2},{4,5},{5,4},{6,7},{7,6},{8,9},{9,8},{10,11... | collective-permute-start | bytes 1179656 | tf_op jit(solution)/shard_map/ppermute | solution.py:138
  80.2 11.6 %collective-permute-start.25 = (bf16[192,1024]{1,0:T(8,128)(2,1)S(1)}, bf16[192,1024]{1,0:T(8,128)(2,1)S(1)}, u32[]{:S(2)}, u32[]{:S(2)}) collective-permute-start(bf16[192,1024]{1,0:T(8,128)(2,1)S(1)} %shard_map.72), channel_id=1, source_target_pairs={{0,1},{1,0},{2,3},{3,2},{4,5},{5,4},{6,7},{7,6},{8,9},{9,8},{10,11... | collective-permute-start | bytes 1179656 | tf_op jit(solution)/shard_map/ppermute | solution.py:138
  89.5 7.8 %collective-permute-start.16 = (bf16[96,1024]{1,0:T(8,128)(2,1)S(1)}, bf16[96,1024]{1,0:T(8,128)(2,1)S(1)}, u32[]{:S(2)}, u32[]{:S(2)}) collective-permute-start(bf16[96,1024]{1,0:T(8,128)(2,1)S(1)} %slice.178), channel_id=1, source_target_pairs={{0,2},{2,0},{4,6},{6,4},{8,10},{10,8},{12,14},{14,12},{1,3},{3,1},... | collective-permute-start | bytes 589832 | tf_op jit(solution)/shard_map/ppermute | solution.py:135
  91.2 10.4 %collective-permute-start.21 = (bf16[96,1024]{1,0:T(8,128)(2,1)S(1)}, bf16[96,1024]{1,0:T(8,128)(2,1)S(1)}, u32[]{:S(2)}, u32[]{:S(2)}) collective-permute-start(bf16[96,1024]{1,0:T(8,128)(2,1)S(1)} %slice.184), channel_id=1, source_target_pairs={{0,2},{2,0},{4,6},{6,4},{8,10},{10,8},{12,14},{14,12},{1,3},{3,1},... | collective-permute-start | bytes 589832 | tf_op jit(solution)/shard_map/ppermute | solution.py:135
  91.9 12.9 %collective-permute-start.26 = (bf16[96,1024]{1,0:T(8,128)(2,1)S(1)}, bf16[96,1024]{1,0:T(8,128)(2,1)S(1)}, u32[]{:S(2)}, u32[]{:S(2)}) collective-permute-start(bf16[96,1024]{1,0:T(8,128)(2,1)S(1)} %slice.190), channel_id=1, source_target_pairs={{0,2},{2,0},{4,6},{6,4},{8,10},{10,8},{12,14},{14,12},{1,3},{3,1},... | collective-permute-start | bytes 589832 | tf_op jit(solution)/shard_map/ppermute | solution.py:135
  97.4 8.7 %collective-permute-start.17 = (bf16[24,1024]{1,0:T(8,128)(2,1)S(1)}, bf16[24,1024]{1,0:T(8,128)(2,1)S(1)}, u32[]{:S(2)}, u32[]{:S(2)}) collective-permute-start(bf16[24,1024]{1,0:T(8,128)(2,1)S(1)} %get-tuple-element.27), channel_id=1, source_target_pairs={{0,12},{2,14},{4,0},{6,2},{8,4},{10,6},{12,8},{14,10},{1,13},{3,15... | collective-permute-start | bytes 147464 | tf_op jit(solution)/shard_map/ppermute | solution.py:132
  97.8 8.3 %collective-permute-start.18 = (bf16[24,1024]{1,0:T(8,128)(2,1)S(1)}, bf16[24,1024]{1,0:T(8,128)(2,1)S(1)}, u32[]{:S(2)}, u32[]{:S(2)}) collective-permute-start(bf16[24,1024]{1,0:T(8,128)(2,1)S(1)} %get-tuple-element.26), channel_id=1, source_target_pairs={{0,8},{2,10},{4,12},{6,14},{8,0},{10,2},{12,4},{14,6},{1,9},{3,11}... | collective-permute-start | bytes 147464 | tf_op jit(solution)/shard_map/ppermute | solution.py:132
  99.0 11.0 %collective-permute-start.19 = (bf16[24,1024]{1,0:T(8,128)(2,1)S(1)}, bf16[24,1024]{1,0:T(8,128)(2,1)S(1)}, u32[]{:S(2)}, u32[]{:S(2)}) collective-permute-start(bf16[24,1024]{1,0:T(8,128)(2,1)S(1)} %get-tuple-element.25), channel_id=1, source_target_pairs={{0,4},{2,6},{4,8},{6,10},{8,12},{10,14},{12,0},{14,2},{1,5},{3,7},... | collective-permute-start | bytes 147464 | tf_op jit(solution)/shard_map/ppermute | solution.py:132
  101.6 8.6 %collective-permute-start.22 = (bf16[24,1024]{1,0:T(8,128)(2,1)S(1)}, bf16[24,1024]{1,0:T(8,128)(2,1)S(1)}, u32[]{:S(2)}, u32[]{:S(2)}) collective-permute-start(bf16[24,1024]{1,0:T(8,128)(2,1)S(1)} %get-tuple-element.31), channel_id=1, source_target_pairs={{0,12},{2,14},{4,0},{6,2},{8,4},{10,6},{12,8},{14,10},{1,13},{3,15... | collective-permute-start | bytes 147464 | tf_op jit(solution)/shard_map/ppermute | solution.py:132
  104.8 6.6 %collective-permute-start.23 = (bf16[24,1024]{1,0:T(8,128)(2,1)S(1)}, bf16[24,1024]{1,0:T(8,128)(2,1)S(1)}, u32[]{:S(2)}, u32[]{:S(2)}) collective-permute-start(bf16[24,1024]{1,0:T(8,128)(2,1)S(1)} %get-tuple-element.30), channel_id=1, source_target_pairs={{0,8},{2,10},{4,12},{6,14},{8,0},{10,2},{12,4},{14,6},{1,9},{3,11}... | collective-permute-start | bytes 147464 | tf_op jit(solution)/shard_map/ppermute | solution.py:132
  (9 other events, 62.1 us)

commit v3 on v2

--- a/solution.py
+++ b/solution.py
@@ -141,29 +141,44 @@
     weights = weights.reshape(D, hid_local // 64, 128)
     outgoing = jnp.dot(pick_matrix, tokens, preferred_element_type=jnp.float32).astype(jnp.bfloat16)
 
-    sums = None
+    def after(x, *others):
+        return lax.optimization_barrier((x,) + others)[0]
+
+    arrived, own = [], []
     for c in range(CHUNKS):
         part = outgoing[:, c * width:(c + 1) * width].reshape(EXP_WIN, CAP, width)
-        arrived = jnp.concatenate([part[0]] + [to_expert(part[d], d) for d in range(1, EXP_WIN)], axis=0)
-        own = jnp.concatenate([arrived] + [to_rank(arrived, d) for d in range(1, slices)], axis=0)
-        other = to_core(own)
+        arrived.append(jnp.concatenate([part[0]] + [to_expert(part[d], d) for d in range(1, EXP_WIN)], axis=0))
+        own.append(jnp.concatenate([arrived[c]] + [to_rank(arrived[c], d) for d in range(1, slices)], axis=0))
+
+    sums = []
+    for c in range(CHUNKS):
+        other = to_core(own[c] if c < 2 else after(own[c], sums[c - 2]))
+        waits = own[c + 1:c + 2] + arrived[c + 2:c + 3]
+        if waits:
+            other = after(other, *waits)
         at = (jnp.stack([core, 1 - core]) * half + c * width) // STEP
-        sums = gate_up(own, other, weights, sums, at.astype(jnp.int32), c == CHUNKS - 1)
-    hidden = sums
-
-    mixed = []
+        before = sums[c - 1] if c else None
+        sums.append(gate_up(own[c], other, weights, before, at.astype(jnp.int32), c == CHUNKS - 1))
+    hidden = sums[-1]
+
+    mixed, shares, totals = [], [], []
     for c in range(CHUNKS):
         tiles = half // COLS
         start = c * (width // COLS)
+        if c:
+            hidden = after(hidden, shares[c - 1], *totals[:c - 1])
         theirs = down(hidden, w_out[0], (1 - core) * tiles + start, width, jnp.bfloat16)
         landed = to_core(theirs)
-        mine = down(hidden, w_out[0], core * tiles + start, width, jnp.float32)
+        mine = down(after(hidden, theirs), w_out[0], core * tiles + start, width, jnp.float32)
         share = (mine + landed.astype(jnp.float32)).astype(jnp.bfloat16)
+        shares.append(share)
         share = share.reshape(slices, EXP_WIN * CAP, width)
         total = share[0].astype(jnp.float32)
         for d in range(1, slices):
             total = total + to_rank(share[d], slices - d).astype(jnp.float32)
-        total = total.astype(jnp.bfloat16).reshape(EXP_WIN, CAP, width)
+        total = total.astype(jnp.bfloat16)
+        totals.append(total)
+        total = total.reshape(EXP_WIN, CAP, width)
         returned = jnp.concatenate([total[0]] + [to_expert(total[d], EXP_WIN - d) for d in range(1, EXP_WIN)], axis=0)
         mixed.append(jnp.dot(
             combine,

time: 118 us -> 114 us (0.966)
  waiting for transfers between devices: 20.2 us -> 17.8 us
  other arithmetic: 3.84 us -> 2.49 us
    ppermute x6, waiting for transfers between devices: 15.1 us -> 9.24 us  [to_rank(): lax.ppermute(x, 'expert', [(e * slices + r, e * slices + (r + d) % slices...]
    ppermute x18, waiting for transfers between devices: 5.03 us -> 7.46 us  [to_expert(): lax.ppermute(x, 'expert', [(e * slices + r, (e + d) % EXP_WIN * slices +...]
    unnamed x16 -> x18, local copies, waits for them, and re-layouts: 2.5 us -> 2.5 us
  transfers between devices with their start and end apart: 30 -> 30, of which waited for: 10 -> 9; matrix products, arithmetic and copies ran while one was open for 3% -> 1% of each run, Pallas kernels for 33% -> 34%
where the time goes in v3:
time: 114 us
  Pallas kernels  53.1 us (47%)
  starting transfers between devices  35.4 us (31%)
  waiting for transfers between devices  17.8 us (16%)
  local copies, waits for them, and re-layouts  3.08 us (3%)
  other arithmetic  2.49 us (2%)
  matrix products  1.63 us (1%)
    pallas_call x3, Pallas kernels, gate_up(): pl.pallas_call(functools.partial(gate_up_body, steps, first, last), grid_...  35.9 us
    ppermute x18, starting transfers between devices, to_expert(): lax.ppermute(x, 'expert', [(e * slices + r, (e + d) % EXP_WIN * slices +...  27.3 us
    pallas_call x6, Pallas kernels, down(): pl.pallas_call(down_body, grid_spec=pltpu.PrefetchScalarGridSpec(num_scal...  17.2 us
    ppermute x6, waiting for transfers between devices, to_rank(): lax.ppermute(x, 'expert', [(e * slices + r, e * slices + (r + d) % slices...  9.24 us
    ppermute x18, waiting for transfers between devices, to_expert(): lax.ppermute(x, 'expert', [(e * slices + r, (e + d) % EXP_WIN * slices +...  7.46 us
    ppermute x6, starting transfers between devices, to_rank(): lax.ppermute(x, 'expert', [(e * slices + r, e * slices + (r + d) % slices...  6.78 us
    unnamed x18, local copies, waits for them, and re-layouts  2.5 us
  transfers between devices with their start and end apart: 30, of which 9 were waited for; matrix products, arithmetic and copies ran while one was open for 1% of the time, Pallas kernels for 34%

profile of v3, /device:TPU:0, one launch (start us, length us, event | category | flops | bytes accessed | tf_op | source)
XLA Modules:
  0.0 114.0 jit_solution(12266863972563268860)
XLA Ops:
  2.7 4.1 %collective-permute-start.10 = (bf16[24,1024]{1,0:T(8,128)(2,1)S(1)}, bf16[24,1024]{1,0:T(8,128)(2,1)S(1)}, u32[]{:S(2)}, u32[]{:S(2)}) collective-permute-start(bf16[24,1024]{1,0:T(8,128)(2,1)S(1)} %get-tuple-element.30), channel_id=1, source_target_pairs={{0,8},{2,10},{4,12},{6,14},{8,0},{10,2},{12,4},{14,6},{1,9},{3,11}... | collective-permute-start | bytes 147464 | tf_op jit(solution)/shard_map/ppermute | solution.py:132
  8.9 1.6 %collective-permute-start = (bf16[24,1024]{1,0:T(8,128)(2,1)S(1)}, bf16[24,1024]{1,0:T(8,128)(2,1)S(1)}, u32[]{:S(2)}, u32[]{:S(2)}) collective-permute-start(bf16[24,1024]{1,0:T(8,128)(2,1)S(1)} %get-tuple-element.38), channel_id=1, source_target_pairs={{0,4},{2,6},{4,8},{6,10},{8,12},{10,14},{12,0},{14,2},{1,5},{3,7},... | collective-permute-start | bytes 147464 | tf_op jit(solution)/shard_map/ppermute | solution.py:132
  10.5 2.1 %collective-permute-start.1 = (bf16[24,1024]{1,0:T(8,128)(2,1)S(1)}, bf16[24,1024]{1,0:T(8,128)(2,1)S(1)}, u32[]{:S(2)}, u32[]{:S(2)}) collective-permute-start(bf16[24,1024]{1,0:T(8,128)(2,1)S(1)} %get-tuple-element.37), channel_id=1, source_target_pairs={{0,8},{2,10},{4,12},{6,14},{8,0},{10,2},{12,4},{14,6},{1,9},{3,11}... | collective-permute-start | bytes 147464 | tf_op jit(solution)/shard_map/ppermute | solution.py:132
  12.7 2.1 %collective-permute-start.2 = (bf16[24,1024]{1,0:T(8,128)(2,1)S(1)}, bf16[24,1024]{1,0:T(8,128)(2,1)S(1)}, u32[]{:S(2)}, u32[]{:S(2)}) collective-permute-start(bf16[24,1024]{1,0:T(8,128)(2,1)S(1)} %get-tuple-element.36), channel_id=1, source_target_pairs={{0,12},{2,14},{4,0},{6,2},{8,4},{10,6},{12,8},{14,10},{1,13},{3,15... | collective-permute-start | bytes 147464 | tf_op jit(solution)/shard_map/ppermute | solution.py:132
  15.6 3.1 %collective-permute-start.6 = (bf16[24,1024]{1,0:T(8,128)(2,1)S(1)}, bf16[24,1024]{1,0:T(8,128)(2,1)S(1)}, u32[]{:S(2)}, u32[]{:S(2)}) collective-permute-start(bf16[24,1024]{1,0:T(8,128)(2,1)S(1)} %get-tuple-element.32), channel_id=1, source_target_pairs={{0,12},{2,14},{4,0},{6,2},{8,4},{10,6},{12,8},{14,10},{1,13},{3,15... | collective-permute-start | bytes 147464 | tf_op jit(solution)/shard_map/ppermute | solution.py:132
  18.7 1.5 %collective-permute-start.12 = (bf16[96,1024]{1,0:T(8,128)(2,1)S(1)}, bf16[96,1024]{1,0:T(8,128)(2,1)S(1)}, u32[]{:S(2)}, u32[]{:S(2)}) collective-permute-start(bf16[96,1024]{1,0:T(8,128)(2,1)S(1)} %pad_maximum_fusion.3), channel_id=1, source_target_pairs={{0,2},{2,0},{4,6},{6,4},{8,10},{10,8},{12,14},{14,12},{1,3},{3,1},... | collective-permute-start | bytes 589832 | tf_op jit(solution)/shard_map/ppermute | solution.py:135
  21.3 1.6 %collective-permute-start.7 = (bf16[96,1024]{1,0:T(8,128)(2,1)S(1)}, bf16[96,1024]{1,0:T(8,128)(2,1)S(1)}, u32[]{:S(2)}, u32[]{:S(2)}) collective-permute-start(bf16[96,1024]{1,0:T(8,128)(2,1)S(1)} %pad_maximum_fusion.2), channel_id=1, source_target_pairs={{0,2},{2,0},{4,6},{6,4},{8,10},{10,8},{12,14},{14,12},{1,3},{3,1},... | collective-permute-start | bytes 589832 | tf_op jit(solution)/shard_map/ppermute | solution.py:135
  23.0 7.5 %collective-permute-done.7 = bf16[96,1024]{1,0:T(8,128)(2,1)S(1)} collective-permute-done((bf16[96,1024]{1,0:T(8,128)(2,1)S(1)}, bf16[96,1024]{1,0:T(8,128)(2,1)S(1)}, u32[]{:S(2)}, u32[]{:S(2)}) %collective-permute-start.7) | collective-permute-done | bytes 196640 | tf_op jit(solution)/shard_map/ppermute | solution.py:135
  32.3 11.6 %shard_map.64.refs_4_ = f32[192,4096]{1,0:T(8,128)S(1)} custom-call(s32[2]{0:T(128)S(1)} %get-tuple-element.52.refs_0_, bf16[192,1024]{1,0:T(8,128)(2,1)S(1)} %constant_dynamic-update-slice_fusion.5.refs_1_, bf16[192,1024]{1,0:T(8,128)(2,1)S(1)} %collective-permute-done.8.refs_2_, bf16[6144,32,128]{2,1,0:T(8,128)(2,1)} %bitcast.25), custom_call_target="tpu_custom_call" | custom-call | flops 3221225472 | bytes 16777216 | tf_op jit(solution)/shard_map/pallas_call | solution.py:59
  43.9 1.6 %copy-done.2 = f32[192,4096]{1,0:T(8,128)} copy-done((f32[192,4096]{1,0:T(8,128)}, f32[192,4096]{1,0:T(8,128)S(1)}, u32[]{:S(2)}) %copy-start.2) | copy-done | bytes 3145752
  45.6 12.6 %shard_map.65.refs_4_ = f32[192,4096]{1,0:T(8,128)S(1)} custom-call(s32[2]{0:T(128)S(1)} %get-tuple-element.23.refs_0_, bf16[192,1024]{1,0:T(8,128)(2,1)S(1)} %constant_dynamic-update-slice_fusion.10.refs_1_, bf16[192,1024]{1,0:T(8,128)(2,1)S(1)} %collective-permute-done.14.refs_2_, bf16[6144,32,128]{2,1,0:T(8,128)(2,1)} %bitcast.26, f32[192,4096]{1,0:T(8,128)} %copy-done.2), custom_call_target="tpu_custom_call" | custom-call | flops 3221225472 | bytes 16777216 | tf_op jit(solution)/shard_map/pallas_call | solution.py:59
  58.2 11.7 %shard_map.66.h_ref = bf16[192,2048]{1,0:T(8,128)(2,1)S(1)} custom-call(s32[2]{0:T(128)S(1)} %get-tuple-element.53.refs_0_, bf16[192,1024]{1,0:T(8,128)(2,1)S(1)} %constant_dynamic-update-slice_fusion.refs_1_, bf16[192,1024]{1,0:T(8,128)(2,1)S(1)} %collective-permute-done.13.refs_2_, bf16[6144,32,128]{2,1,0:T(8,128)(2,1)} %bitcast.27, ...), custom_call_target="tpu_custom_call" | custom-call | flops 3221225472 | bytes 16777216 | tf_op jit(solution)/shard_map/pallas_call | solution.py:59
  69.9 2.9 %shard_map.67 = bf16[192,1024]{1,0:T(8,128)(2,1)S(1)} custom-call(s32[1]{0:T(128)} %bitcast.9.at_ref, bf16[192,2048]{1,0:T(8,128)(2,1)S(1)} %shard_map.66.h_ref, bf16[2048,6144]{1,0:T(8,128)(2,1)} %bitcast.19), custom_call_target="tpu_custom_call" | custom-call | flops 805306368 | bytes 4194304 | tf_op jit(solution)/shard_map/pallas_call | solution.py:80
  73.5 2.9 %shard_map.68 = f32[192,1024]{1,0:T(8,128)S(1)} custom-call(s32[1]{0:T(128)} %bitcast.1.at_ref, bf16[192,2048]{1,0:T(8,128)(2,1)S(1)} %shard_map.66.h_ref, bf16[2048,6144]{1,0:T(8,128)(2,1)} %bitcast.20), custom_call_target="tpu_custom_call" | custom-call | flops 805306368 | bytes 4194304 | tf_op jit(solution)/shard_map/pallas_call | solution.py:80
  76.5 1.6 %collective-permute-start.16 = (bf16[96,1024]{1,0:T(8,128)(2,1)S(1)}, bf16[96,1024]{1,0:T(8,128)(2,1)S(1)}, u32[]{:S(2)}, u32[]{:S(2)}) collective-permute-start(bf16[96,1024]{1,0:T(8,128)(2,1)S(1)} %slice.178), channel_id=1, source_target_pairs={{0,2},{2,0},{4,6},{6,4},{8,10},{10,8},{12,14},{14,12},{1,3},{3,1},... | collective-permute-start | bytes 589832 | tf_op jit(solution)/shard_map/ppermute | solution.py:135
  78.4 2.9 %shard_map.69 = bf16[192,1024]{1,0:T(8,128)(2,1)S(1)} custom-call(s32[1]{0:T(128)} %bitcast.12.at_ref, bf16[192,2048]{1,0:T(8,128)(2,1)S(1)} %shard_map.66.h_ref, bf16[2048,6144]{1,0:T(8,128)(2,1)} %bitcast.21), custom_call_target="tpu_custom_call" | custom-call | flops 805306368 | bytes 4194304 | tf_op jit(solution)/shard_map/pallas_call | solution.py:80
  81.4 2.9 %shard_map.70 = f32[192,1024]{1,0:T(8,128)S(1)} custom-call(s32[1]{0:T(128)} %bitcast.11.at_ref, bf16[192,2048]{1,0:T(8,128)(2,1)S(1)} %shard_map.66.h_ref, bf16[2048,6144]{1,0:T(8,128)(2,1)} %bitcast.22), custom_call_target="tpu_custom_call" | custom-call | flops 805306368 | bytes 4194304 | tf_op jit(solution)/shard_map/pallas_call | solution.py:80
  84.3 2.9 %collective-permute-start.17 = (bf16[24,1024]{1,0:T(8,128)(2,1)S(1)}, bf16[24,1024]{1,0:T(8,128)(2,1)S(1)}, u32[]{:S(2)}, u32[]{:S(2)}) collective-permute-start(bf16[24,1024]{1,0:T(8,128)(2,1)S(1)} %get-tuple-element.43), channel_id=1, source_target_pairs={{0,12},{2,14},{4,0},{6,2},{8,4},{10,6},{12,8},{14,10},{1,13},{3,15... | collective-permute-start | bytes 147464 | tf_op jit(solution)/shard_map/ppermute | solution.py:132
  89.1 2.8 %shard_map.71 = bf16[192,1024]{1,0:T(8,128)(2,1)S(1)} custom-call(s32[1]{0:T(128)} %bitcast.14.at_ref, bf16[192,2048]{1,0:T(8,128)(2,1)S(1)} %shard_map.66.h_ref, bf16[2048,6144]{1,0:T(8,128)(2,1)} %bitcast.23), custom_call_target="tpu_custom_call" | custom-call | flops 805306368 | bytes 4194304 | tf_op jit(solution)/shard_map/pallas_call | solution.py:80
  93.6 2.9 %shard_map.72 = f32[192,1024]{1,0:T(8,128)S(1)} custom-call(s32[1]{0:T(128)} %bitcast.13.at_ref, bf16[192,2048]{1,0:T(8,128)(2,1)S(1)} %shard_map.66.h_ref, bf16[2048,6144]{1,0:T(8,128)(2,1)} %bitcast.24), custom_call_target="tpu_custom_call" | custom-call | flops 805306368 | bytes 4194304 | tf_op jit(solution)/shard_map/pallas_call | solution.py:80
  97.5 2.4 %collective-permute-start.22 = (bf16[24,1024]{1,0:T(8,128)(2,1)S(1)}, bf16[24,1024]{1,0:T(8,128)(2,1)S(1)}, u32[]{:S(2)}, u32[]{:S(2)}) collective-permute-start(bf16[24,1024]{1,0:T(8,128)(2,1)S(1)} %get-tuple-element.47), channel_id=1, source_target_pairs={{0,12},{2,14},{4,0},{6,2},{8,4},{10,6},{12,8},{14,10},{1,13},{3,15... | collective-permute-start | bytes 147464 | tf_op jit(solution)/shard_map/ppermute | solution.py:132
  101.0 1.7 %collective-permute-done.26 = bf16[96,1024]{1,0:T(8,128)(2,1)S(1)} collective-permute-done((bf16[96,1024]{1,0:T(8,128)(2,1)S(1)}, bf16[96,1024]{1,0:T(8,128)(2,1)S(1)}, u32[]{:S(2)}, u32[]{:S(2)}) %collective-permute-start.26) | collective-permute-done | bytes 196640 | tf_op jit(solution)/shard_map/ppermute | solution.py:135
  102.9 3.1 %collective-permute-start.27 = (bf16[24,1024]{1,0:T(8,128)(2,1)S(1)}, bf16[24,1024]{1,0:T(8,128)(2,1)S(1)}, u32[]{:S(2)}, u32[]{:S(2)}) collective-permute-start(bf16[24,1024]{1,0:T(8,128)(2,1)S(1)} %get-tuple-element.51), channel_id=1, source_target_pairs={{0,12},{2,14},{4,0},{6,2},{8,4},{10,6},{12,8},{14,10},{1,13},{3,15... | collective-permute-start | bytes 147464 | tf_op jit(solution)/shard_map/ppermute | solution.py:132
  108.0 3.6 %collective-permute-done.28 = bf16[24,1024]{1,0:T(8,128)(2,1)S(1)} collective-permute-done((bf16[24,1024]{1,0:T(8,128)(2,1)S(1)}, bf16[24,1024]{1,0:T(8,128)(2,1)S(1)}, u32[]{:S(2)}, u32[]{:S(2)}) %collective-permute-start.28) | collective-permute-done | bytes 49184 | tf_op jit(solution)/shard_map/ppermute | solution.py:132
  (100 shorter events, 20.0 us)
Async XLA Ops:
  2.7 9.9 %collective-permute-start.10 = (bf16[24,1024]{1,0:T(8,128)(2,1)S(1)}, bf16[24,1024]{1,0:T(8,128)(2,1)S(1)}, u32[]{:S(2)}, u32[]{:S(2)}) collective-permute-start(bf16[24,1024]{1,0:T(8,128)(2,1)S(1)} %get-tuple-element.30), channel_id=1, source_target_pairs={{0,8},{2,10},{4,12},{6,14},{8,0},{10,2},{12,4},{14,6},{1,9},{3,11}... | collective-permute-start | bytes 147464 | tf_op jit(solution)/shard_map/ppermute | solution.py:132
  6.8 7.9 %collective-permute-start.11 = (bf16[24,1024]{1,0:T(8,128)(2,1)S(1)}, bf16[24,1024]{1,0:T(8,128)(2,1)S(1)}, u32[]{:S(2)}, u32[]{:S(2)}) collective-permute-start(bf16[24,1024]{1,0:T(8,128)(2,1)S(1)} %get-tuple-element.29), channel_id=1, source_target_pairs={{0,12},{2,14},{4,0},{6,2},{8,4},{10,6},{12,8},{14,10},{1,13},{3,15... | collective-permute-start | bytes 147464 | tf_op jit(solution)/shard_map/ppermute | solution.py:132
  8.2 6.6 %collective-permute-start.9 = (bf16[24,1024]{1,0:T(8,128)(2,1)S(1)}, bf16[24,1024]{1,0:T(8,128)(2,1)S(1)}, u32[]{:S(2)}, u32[]{:S(2)}) collective-permute-start(bf16[24,1024]{1,0:T(8,128)(2,1)S(1)} %get-tuple-element.31), channel_id=1, source_target_pairs={{0,4},{2,6},{4,8},{6,10},{8,12},{10,14},{12,0},{14,2},{1,5},{3,7},... | collective-permute-start | bytes 147464 | tf_op jit(solution)/shard_map/ppermute | solution.py:132
  8.9 6.7 %collective-permute-start = (bf16[24,1024]{1,0:T(8,128)(2,1)S(1)}, bf16[24,1024]{1,0:T(8,128)(2,1)S(1)}, u32[]{:S(2)}, u32[]{:S(2)}) collective-permute-start(bf16[24,1024]{1,0:T(8,128)(2,1)S(1)} %get-tuple-element.38), channel_id=1, source_target_pairs={{0,4},{2,6},{4,8},{6,10},{8,12},{10,14},{12,0},{14,2},{1,5},{3,7},... | collective-permute-start | bytes 147464 | tf_op jit(solution)/shard_map/ppermute | solution.py:132
  10.5 8.2 %collective-permute-start.1 = (bf16[24,1024]{1,0:T(8,128)(2,1)S(1)}, bf16[24,1024]{1,0:T(8,128)(2,1)S(1)}, u32[]{:S(2)}, u32[]{:S(2)}) collective-permute-start(bf16[24,1024]{1,0:T(8,128)(2,1)S(1)} %get-tuple-element.37), channel_id=1, source_target_pairs={{0,8},{2,10},{4,12},{6,14},{8,0},{10,2},{12,4},{14,6},{1,9},{3,11}... | collective-permute-start | bytes 147464 | tf_op jit(solution)/shard_map/ppermute | solution.py:132
  12.7 7.5 %collective-permute-start.2 = (bf16[24,1024]{1,0:T(8,128)(2,1)S(1)}, bf16[24,1024]{1,0:T(8,128)(2,1)S(1)}, u32[]{:S(2)}, u32[]{:S(2)}) collective-permute-start(bf16[24,1024]{1,0:T(8,128)(2,1)S(1)} %get-tuple-element.36), channel_id=1, source_target_pairs={{0,12},{2,14},{4,0},{6,2},{8,4},{10,6},{12,8},{14,10},{1,13},{3,15... | collective-permute-start | bytes 147464 | tf_op jit(solution)/shard_map/ppermute | solution.py:132
  14.8 6.0 %collective-permute-start.4 = (bf16[24,1024]{1,0:T(8,128)(2,1)S(1)}, bf16[24,1024]{1,0:T(8,128)(2,1)S(1)}, u32[]{:S(2)}, u32[]{:S(2)}) collective-permute-start(bf16[24,1024]{1,0:T(8,128)(2,1)S(1)} %get-tuple-element.34), channel_id=1, source_target_pairs={{0,4},{2,6},{4,8},{6,10},{8,12},{10,14},{12,0},{14,2},{1,5},{3,7},... | collective-permute-start | bytes 147464 | tf_op jit(solution)/shard_map/ppermute | solution.py:132
  14.8 6.0 %collective-permute-start.5 = (bf16[24,1024]{1,0:T(8,128)(2,1)S(1)}, bf16[24,1024]{1,0:T(8,128)(2,1)S(1)}, u32[]{:S(2)}, u32[]{:S(2)}) collective-permute-start(bf16[24,1024]{1,0:T(8,128)(2,1)S(1)} %get-tuple-element.33), channel_id=1, source_target_pairs={{0,8},{2,10},{4,12},{6,14},{8,0},{10,2},{12,4},{14,6},{1,9},{3,11}... | collective-permute-start | bytes 147464 | tf_op jit(solution)/shard_map/ppermute | solution.py:132
  18.7 11.9 %collective-permute-start.12 = (bf16[96,1024]{1,0:T(8,128)(2,1)S(1)}, bf16[96,1024]{1,0:T(8,128)(2,1)S(1)}, u32[]{:S(2)}, u32[]{:S(2)}) collective-permute-start(bf16[96,1024]{1,0:T(8,128)(2,1)S(1)} %pad_maximum_fusion.3), channel_id=1, source_target_pairs={{0,2},{2,0},{4,6},{6,4},{8,10},{10,8},{12,14},{14,12},{1,3},{3,1},... | collective-permute-start | bytes 589832 | tf_op jit(solution)/shard_map/ppermute | solution.py:135
  20.2 11.0 %collective-permute-start.3 = (bf16[96,1024]{1,0:T(8,128)(2,1)S(1)}, bf16[96,1024]{1,0:T(8,128)(2,1)S(1)}, u32[]{:S(2)}, u32[]{:S(2)}) collective-permute-start(bf16[96,1024]{1,0:T(8,128)(2,1)S(1)} %pad_maximum_fusion.1), channel_id=1, source_target_pairs={{0,2},{2,0},{4,6},{6,4},{8,10},{10,8},{12,14},{14,12},{1,3},{3,1},... | collective-permute-start | bytes 589832 | tf_op jit(solution)/shard_map/ppermute | solution.py:135
  21.3 9.1 %collective-permute-start.7 = (bf16[96,1024]{1,0:T(8,128)(2,1)S(1)}, bf16[96,1024]{1,0:T(8,128)(2,1)S(1)}, u32[]{:S(2)}, u32[]{:S(2)}) collective-permute-start(bf16[96,1024]{1,0:T(8,128)(2,1)S(1)} %pad_maximum_fusion.2), channel_id=1, source_target_pairs={{0,2},{2,0},{4,6},{6,4},{8,10},{10,8},{12,14},{14,12},{1,3},{3,1},... | collective-permute-start | bytes 589832 | tf_op jit(solution)/shard_map/ppermute | solution.py:135
  30.6 15.0 %collective-permute-start.14 = (bf16[192,1024]{1,0:T(8,128)(2,1)S(1)}, bf16[192,1024]{1,0:T(8,128)(2,1)S(1)}, u32[]{:S(2)}, u32[]{:S(2)}) collective-permute-start(bf16[192,1024]{1,0:T(8,128)(2,1)S(1)} %constant_dynamic-update-slice_fusion.10.refs_1_), channel_id=1, source_target_pairs={{0,1},{1,0},{2,3},{3,2},{4,5},{5,4},{6,7},{7,6},{8,9},{9,8},{10,11... | collective-permute-start | bytes 1179656 | tf_op jit(solution)/shard_map/ppermute | solution.py:138
  45.5 12.7 %collective-permute-start.13 = (bf16[192,1024]{1,0:T(8,128)(2,1)S(1)}, bf16[192,1024]{1,0:T(8,128)(2,1)S(1)}, u32[]{:S(2)}, u32[]{:S(2)}) collective-permute-start(bf16[192,1024]{1,0:T(8,128)(2,1)S(1)} %constant_dynamic-update-slice_fusion.refs_1_), channel_id=1, source_target_pairs={{0,1},{1,0},{2,3},{3,2},{4,5},{5,4},{6,7},{7,6},{8,9},{9,8},{10,11... | collective-permute-start | bytes 1179656 | tf_op jit(solution)/shard_map/ppermute | solution.py:138
  76.5 7.7 %collective-permute-start.16 = (bf16[96,1024]{1,0:T(8,128)(2,1)S(1)}, bf16[96,1024]{1,0:T(8,128)(2,1)S(1)}, u32[]{:S(2)}, u32[]{:S(2)}) collective-permute-start(bf16[96,1024]{1,0:T(8,128)(2,1)S(1)} %slice.178), channel_id=1, source_target_pairs={{0,2},{2,0},{4,6},{6,4},{8,10},{10,8},{12,14},{14,12},{1,3},{3,1},... | collective-permute-start | bytes 589832 | tf_op jit(solution)/shard_map/ppermute | solution.py:135
  81.3 6.8 %collective-permute-start.20 = (bf16[192,1024]{1,0:T(8,128)(2,1)S(1)}, bf16[192,1024]{1,0:T(8,128)(2,1)S(1)}, u32[]{:S(2)}, u32[]{:S(2)}) collective-permute-start(bf16[192,1024]{1,0:T(8,128)(2,1)S(1)} %shard_map.69), channel_id=1, source_target_pairs={{0,1},{1,0},{2,3},{3,2},{4,5},{5,4},{6,7},{7,6},{8,9},{9,8},{10,11... | collective-permute-start | bytes 1179656 | tf_op jit(solution)/shard_map/ppermute | solution.py:138
  84.3 7.7 %collective-permute-start.17 = (bf16[24,1024]{1,0:T(8,128)(2,1)S(1)}, bf16[24,1024]{1,0:T(8,128)(2,1)S(1)}, u32[]{:S(2)}, u32[]{:S(2)}) collective-permute-start(bf16[24,1024]{1,0:T(8,128)(2,1)S(1)} %get-tuple-element.43), channel_id=1, source_target_pairs={{0,12},{2,14},{4,0},{6,2},{8,4},{10,6},{12,8},{14,10},{1,13},{3,15... | collective-permute-start | bytes 147464 | tf_op jit(solution)/shard_map/ppermute | solution.py:132
  87.3 6.0 %collective-permute-start.18 = (bf16[24,1024]{1,0:T(8,128)(2,1)S(1)}, bf16[24,1024]{1,0:T(8,128)(2,1)S(1)}, u32[]{:S(2)}, u32[]{:S(2)}) collective-permute-start(bf16[24,1024]{1,0:T(8,128)(2,1)S(1)} %get-tuple-element.42), channel_id=1, source_target_pairs={{0,8},{2,10},{4,12},{6,14},{8,0},{10,2},{12,4},{14,6},{1,9},{3,11}... | collective-permute-start | bytes 147464 | tf_op jit(solution)/shard_map/ppermute | solution.py:132
  87.3 6.0 %collective-permute-start.19 = (bf16[24,1024]{1,0:T(8,128)(2,1)S(1)}, bf16[24,1024]{1,0:T(8,128)(2,1)S(1)}, u32[]{:S(2)}, u32[]{:S(2)}) collective-permute-start(bf16[24,1024]{1,0:T(8,128)(2,1)S(1)} %get-tuple-element.41), channel_id=1, source_target_pairs={{0,4},{2,6},{4,8},{6,10},{8,12},{10,14},{12,0},{14,2},{1,5},{3,7},... | collective-permute-start | bytes 147464 | tf_op jit(solution)/shard_map/ppermute | solution.py:132
  88.2 8.3 %collective-permute-start.21 = (bf16[96,1024]{1,0:T(8,128)(2,1)S(1)}, bf16[96,1024]{1,0:T(8,128)(2,1)S(1)}, u32[]{:S(2)}, u32[]{:S(2)}) collective-permute-start(bf16[96,1024]{1,0:T(8,128)(2,1)S(1)} %slice.184), channel_id=1, source_target_pairs={{0,2},{2,0},{4,6},{6,4},{8,10},{10,8},{12,14},{14,12},{1,3},{3,1},... | collective-permute-start | bytes 589832 | tf_op jit(solution)/shard_map/ppermute | solution.py:135
  96.7 6.0 %collective-permute-start.26 = (bf16[96,1024]{1,0:T(8,128)(2,1)S(1)}, bf16[96,1024]{1,0:T(8,128)(2,1)S(1)}, u32[]{:S(2)}, u32[]{:S(2)}) collective-permute-start(bf16[96,1024]{1,0:T(8,128)(2,1)S(1)} %slice.190), channel_id=1, source_target_pairs={{0,2},{2,0},{4,6},{6,4},{8,10},{10,8},{12,14},{14,12},{1,3},{3,1},... | collective-permute-start | bytes 589832 | tf_op jit(solution)/shard_map/ppermute | solution.py:135
  97.5 9.6 %collective-permute-start.22 = (bf16[24,1024]{1,0:T(8,128)(2,1)S(1)}, bf16[24,1024]{1,0:T(8,128)(2,1)S(1)}, u32[]{:S(2)}, u32[]{:S(2)}) collective-permute-start(bf16[24,1024]{1,0:T(8,128)(2,1)S(1)} %get-tuple-element.47), channel_id=1, source_target_pairs={{0,12},{2,14},{4,0},{6,2},{8,4},{10,6},{12,8},{14,10},{1,13},{3,15... | collective-permute-start | bytes 147464 | tf_op jit(solution)/shard_map/ppermute | solution.py:132
  99.8 7.2 %collective-permute-start.23 = (bf16[24,1024]{1,0:T(8,128)(2,1)S(1)}, bf16[24,1024]{1,0:T(8,128)(2,1)S(1)}, u32[]{:S(2)}, u32[]{:S(2)}) collective-permute-start(bf16[24,1024]{1,0:T(8,128)(2,1)S(1)} %get-tuple-element.46), channel_id=1, source_target_pairs={{0,8},{2,10},{4,12},{6,14},{8,0},{10,2},{12,4},{14,6},{1,9},{3,11}... | collective-permute-start | bytes 147464 | tf_op jit(solution)/shard_map/ppermute | solution.py:132
  101.0 6.3 %collective-permute-start.24 = (bf16[24,1024]{1,0:T(8,128)(2,1)S(1)}, bf16[24,1024]{1,0:T(8,128)(2,1)S(1)}, u32[]{:S(2)}, u32[]{:S(2)}) collective-permute-start(bf16[24,1024]{1,0:T(8,128)(2,1)S(1)} %get-tuple-element.45), channel_id=1, source_target_pairs={{0,4},{2,6},{4,8},{6,10},{8,12},{10,14},{12,0},{14,2},{1,5},{3,7},... | collective-permute-start | bytes 147464 | tf_op jit(solution)/shard_map/ppermute | solution.py:132
  107.1 5.9 %collective-permute-start.29 = (bf16[24,1024]{1,0:T(8,128)(2,1)S(1)}, bf16[24,1024]{1,0:T(8,128)(2,1)S(1)}, u32[]{:S(2)}, u32[]{:S(2)}) collective-permute-start(bf16[24,1024]{1,0:T(8,128)(2,1)S(1)} %get-tuple-element.49), channel_id=1, source_target_pairs={{0,4},{2,6},{4,8},{6,10},{8,12},{10,14},{12,0},{14,2},{1,5},{3,7},... | collective-permute-start | bytes 147464 | tf_op jit(solution)/shard_map/ppermute | solution.py:132
  (10 other events, 54.1 us)

commit v4 on v3

--- a/solution.py
+++ b/solution.py
@@ -11,7 +11,7 @@
 EXP_WIN = 4
 CAP = 24
 
-CHUNKS = 3
+CHUNKS = 2
 STEP = 512
 COLS = 512
 

time: 114 us -> 106 us (0.930)
  starting transfers between devices: 35.4 us -> 30.3 us
  Pallas kernels: 53.1 us -> 49.6 us
  waiting for transfers between devices: 17.8 us -> 20.1 us
  local copies, waits for them, and re-layouts: 3.08 us -> 1.43 us
    pallas_call x3 -> x2, Pallas kernels: 35.9 us -> 31.9 us  [gate_up(): pl.pallas_call(functools.partial(gate_up_body, steps, first, last), grid_...]
    ppermute x18 -> x12, waiting for transfers between devices: 7.46 us -> 11.3 us  [to_expert(): lax.ppermute(x, 'expert', [(e * slices + r, (e + d) % EXP_WIN * slices +...]
    ppermute x18 -> x12, starting transfers between devices: 27.3 us -> 24.5 us  [to_expert(): lax.ppermute(x, 'expert', [(e * slices + r, (e + d) % EXP_WIN * slices +...]
    ppermute x6 -> x4, starting transfers between devices: 6.78 us -> 4.97 us  [to_rank(): lax.ppermute(x, 'expert', [(e * slices + r, e * slices + (r + d) % slices...]
    unnamed x18 -> x13, local copies, waits for them, and re-layouts: 2.5 us -> 0.88 us
    pallas_call x6 -> x4, Pallas kernels: 17.2 us -> 17.7 us  [down(): pl.pallas_call(down_body, grid_spec=pltpu.PrefetchScalarGridSpec(num_scal...]
    ppermute x6 -> x4, waiting for transfers between devices: 9.24 us -> 8.81 us  [to_rank(): lax.ppermute(x, 'expert', [(e * slices + r, e * slices + (r + d) % slices...]
  transfers between devices with their start and end apart: 30 -> 20, of which waited for: 9 -> 8; matrix products, arithmetic and copies ran while one was open for 1% -> 1% of each run, Pallas kernels for 34% -> 28%
where the time goes in v4:
time: 106 us
  Pallas kernels  49.6 us (47%)
  starting transfers between devices  30.3 us (29%)
  waiting for transfers between devices  20.1 us (19%)
  other arithmetic  2.45 us (2%)
  matrix products  1.46 us (1%)
  local copies, waits for them, and re-layouts  1.43 us (1%)
    pallas_call x2, Pallas kernels, gate_up(): pl.pallas_call(functools.partial(gate_up_body, steps, first, last), grid_...  31.9 us
    ppermute x12, starting transfers between devices, to_expert(): lax.ppermute(x, 'expert', [(e * slices + r, (e + d) % EXP_WIN * slices +...  24.5 us
    pallas_call x4, Pallas kernels, down(): pl.pallas_call(down_body, grid_spec=pltpu.PrefetchScalarGridSpec(num_scal...  17.7 us
    ppermute x12, waiting for transfers between devices, to_expert(): lax.ppermute(x, 'expert', [(e * slices + r, (e + d) % EXP_WIN * slices +...  11.3 us
    ppermute x4, waiting for transfers between devices, to_rank(): lax.ppermute(x, 'expert', [(e * slices + r, e * slices + (r + d) % slices...  8.81 us
    ppermute x4, starting transfers between devices, to_rank(): lax.ppermute(x, 'expert', [(e * slices + r, e * slices + (r + d) % slices...  4.97 us
  transfers between devices with their start and end apart: 20, of which 8 were waited for; matrix products, arithmetic and copies ran while one was open for 1% of the time, Pallas kernels for 28%

profile of v4, /device:TPU:0, one launch (start us, length us, event | category | flops | bytes accessed | tf_op | source)
XLA Modules:
  0.0 105.7 jit_solution(17393228778844141679)
XLA Ops:
  1.2 0.8 select_reduce_fusion
  2.7 3.1 %collective-permute-start.5 = (bf16[24,1536]{1,0:T(8,128)(2,1)S(1)}, bf16[24,1536]{1,0:T(8,128)(2,1)S(1)}, u32[]{:S(2)}, u32[]{:S(2)}) collective-permute-start(bf16[24,1536]{1,0:T(8,128)(2,1)S(1)} %get-tuple-element.22), channel_id=1, source_target_pairs={{0,4},{2,6},{4,8},{6,10},{8,12},{10,14},{12,0},{14,2},{1,5},{3,7},... | collective-permute-start | bytes 221192 | tf_op jit(solution)/shard_map/ppermute | solution.py:132
  5.8 2.6 %collective-permute-start.6 = (bf16[24,1536]{1,0:T(8,128)(2,1)S(1)}, bf16[24,1536]{1,0:T(8,128)(2,1)S(1)}, u32[]{:S(2)}, u32[]{:S(2)}) collective-permute-start(bf16[24,1536]{1,0:T(8,128)(2,1)S(1)} %get-tuple-element.21), channel_id=1, source_target_pairs={{0,8},{2,10},{4,12},{6,14},{8,0},{10,2},{12,4},{14,6},{1,9},{3,11}... | collective-permute-start | bytes 221192 | tf_op jit(solution)/shard_map/ppermute | solution.py:132
  8.4 1.3 %collective-permute-start.7 = (bf16[24,1536]{1,0:T(8,128)(2,1)S(1)}, bf16[24,1536]{1,0:T(8,128)(2,1)S(1)}, u32[]{:S(2)}, u32[]{:S(2)}) collective-permute-start(bf16[24,1536]{1,0:T(8,128)(2,1)S(1)} %get-tuple-element.20), channel_id=1, source_target_pairs={{0,12},{2,14},{4,0},{6,2},{8,4},{10,6},{12,8},{14,10},{1,13},{3,15... | collective-permute-start | bytes 221192 | tf_op jit(solution)/shard_map/ppermute | solution.py:132
  10.8 2.9 %collective-permute-start.2 = (bf16[24,1536]{1,0:T(8,128)(2,1)S(1)}, bf16[24,1536]{1,0:T(8,128)(2,1)S(1)}, u32[]{:S(2)}, u32[]{:S(2)}) collective-permute-start(bf16[24,1536]{1,0:T(8,128)(2,1)S(1)} %get-tuple-element.23), channel_id=1, source_target_pairs={{0,12},{2,14},{4,0},{6,2},{8,4},{10,6},{12,8},{14,10},{1,13},{3,15... | collective-permute-start | bytes 221192 | tf_op jit(solution)/shard_map/ppermute | solution.py:132
  14.5 1.1 %collective-permute-start.8 = (bf16[96,1536]{1,0:T(8,128)(2,1)S(1)}, bf16[96,1536]{1,0:T(8,128)(2,1)S(1)}, u32[]{:S(2)}, u32[]{:S(2)}) collective-permute-start(bf16[96,1536]{1,0:T(8,128)(2,1)S(1)} %pad_maximum_fusion.2), channel_id=1, source_target_pairs={{0,2},{2,0},{4,6},{6,4},{8,10},{10,8},{12,14},{14,12},{1,3},{3,1},... | collective-permute-start | bytes 884744 | tf_op jit(solution)/shard_map/ppermute | solution.py:135
  15.5 1.1 %collective-permute-done = bf16[24,1536]{1,0:T(8,128)(2,1)S(1)} collective-permute-done((bf16[24,1536]{1,0:T(8,128)(2,1)S(1)}, bf16[24,1536]{1,0:T(8,128)(2,1)S(1)}, u32[]{:S(2)}, u32[]{:S(2)}) %collective-permute-start) | collective-permute-done | bytes 73760 | tf_op jit(solution)/shard_map/ppermute | solution.py:132
  16.6 3.0 %collective-permute-done.1 = bf16[24,1536]{1,0:T(8,128)(2,1)S(1)} collective-permute-done((bf16[24,1536]{1,0:T(8,128)(2,1)S(1)}, bf16[24,1536]{1,0:T(8,128)(2,1)S(1)}, u32[]{:S(2)}, u32[]{:S(2)}) %collective-permute-start.1) | collective-permute-done | bytes 73760 | tf_op jit(solution)/shard_map/ppermute | solution.py:132
  19.7 1.7 %collective-permute-start.3 = (bf16[96,1536]{1,0:T(8,128)(2,1)S(1)}, bf16[96,1536]{1,0:T(8,128)(2,1)S(1)}, u32[]{:S(2)}, u32[]{:S(2)}) collective-permute-start(bf16[96,1536]{1,0:T(8,128)(2,1)S(1)} %pad_maximum_fusion.1), channel_id=1, source_target_pairs={{0,2},{2,0},{4,6},{6,4},{8,10},{10,8},{12,14},{14,12},{1,3},{3,1},... | collective-permute-start | bytes 884744 | tf_op jit(solution)/shard_map/ppermute | solution.py:135
  22.4 6.2 %collective-permute-done.3 = bf16[96,1536]{1,0:T(8,128)(2,1)S(1)} collective-permute-done((bf16[96,1536]{1,0:T(8,128)(2,1)S(1)}, bf16[96,1536]{1,0:T(8,128)(2,1)S(1)}, u32[]{:S(2)}, u32[]{:S(2)}) %collective-permute-start.3) | collective-permute-done | bytes 294944 | tf_op jit(solution)/shard_map/ppermute | solution.py:135
  28.7 15.9 %shard_map.64.refs_4_ = f32[192,4096]{1,0:T(8,128)S(1)} custom-call(s32[2]{0:T(128)S(1)} %get-tuple-element.15.refs_0_, bf16[192,1536]{1,0:T(8,128)(2,1)S(1)} %constant_dynamic-update-slice_fusion.5.refs_1_, bf16[192,1536]{1,0:T(8,128)(2,1)S(1)} %collective-permute-done.9.refs_2_, bf16[6144,32,128]{2,1,0:T(8,128)(2,1)} %bitcast.20), custom_call_target="tpu_custom_call" | custom-call | flops 4831838208 | bytes 25165824 | tf_op jit(solution)/shard_map/pallas_call | solution.py:59
  44.7 15.9 %shard_map.65.h_ref = bf16[192,2048]{1,0:T(8,128)(2,1)S(1)} custom-call(s32[2]{0:T(128)S(1)} %and_select_fusion.1.refs_0_, bf16[192,1536]{1,0:T(8,128)(2,1)S(1)} %constant_dynamic-update-slice_fusion.refs_1_, bf16[192,1536]{1,0:T(8,128)(2,1)S(1)} %collective-permute-done.4.refs_2_, bf16[6144,32,128]{2,1,0:T(8,128)(2,1)} %bitcast.21, ...), custom_call_target="tpu_custom_call" | custom-call | flops 4831838208 | bytes 25165824 | tf_op jit(solution)/shard_map/pallas_call | solution.py:59
  60.7 4.4 %shard_map.66 = bf16[192,1536]{1,0:T(8,128)(2,1)S(1)} custom-call(s32[1]{0:T(128)} %bitcast.9.at_ref, bf16[192,2048]{1,0:T(8,128)(2,1)S(1)} %shard_map.65.h_ref, bf16[2048,6144]{1,0:T(8,128)(2,1)} %bitcast.16), custom_call_target="tpu_custom_call" | custom-call | flops 1207959552 | bytes 6291456 | tf_op jit(solution)/shard_map/pallas_call | solution.py:80
  65.9 4.4 %shard_map.67 = f32[192,1536]{1,0:T(8,128)S(1)} custom-call(s32[1]{0:T(128)} %bitcast.1.at_ref, bf16[192,2048]{1,0:T(8,128)(2,1)S(1)} %shard_map.65.h_ref, bf16[2048,6144]{1,0:T(8,128)(2,1)} %bitcast.17), custom_call_target="tpu_custom_call" | custom-call | flops 1207959552 | bytes 6291456 | tf_op jit(solution)/shard_map/pallas_call | solution.py:80
  70.5 1.4 %collective-permute-start.11 = (bf16[96,1536]{1,0:T(8,128)(2,1)S(1)}, bf16[96,1536]{1,0:T(8,128)(2,1)S(1)}, u32[]{:S(2)}, u32[]{:S(2)}) collective-permute-start(bf16[96,1536]{1,0:T(8,128)(2,1)S(1)} %slice.119), channel_id=1, source_target_pairs={{0,2},{2,0},{4,6},{6,4},{8,10},{10,8},{12,14},{14,12},{1,3},{3,1},... | collective-permute-start | bytes 884744 | tf_op jit(solution)/shard_map/ppermute | solution.py:135
  72.2 4.4 %shard_map.68 = bf16[192,1536]{1,0:T(8,128)(2,1)S(1)} custom-call(s32[1]{0:T(128)} %bitcast.12.at_ref, bf16[192,2048]{1,0:T(8,128)(2,1)S(1)} %shard_map.65.h_ref, bf16[2048,6144]{1,0:T(8,128)(2,1)} %bitcast.18), custom_call_target="tpu_custom_call" | custom-call | flops 1207959552 | bytes 6291456 | tf_op jit(solution)/shard_map/pallas_call | solution.py:80
  76.7 4.4 %shard_map.69 = f32[192,1536]{1,0:T(8,128)S(1)} custom-call(s32[1]{0:T(128)} %bitcast.11.at_ref, bf16[192,2048]{1,0:T(8,128)(2,1)S(1)} %shard_map.65.h_ref, bf16[2048,6144]{1,0:T(8,128)(2,1)} %bitcast.19), custom_call_target="tpu_custom_call" | custom-call | flops 1207959552 | bytes 6291456 | tf_op jit(solution)/shard_map/pallas_call | solution.py:80
  82.2 5.3 %collective-permute-start.12 = (bf16[24,1536]{1,0:T(8,128)(2,1)S(1)}, bf16[24,1536]{1,0:T(8,128)(2,1)S(1)}, u32[]{:S(2)}, u32[]{:S(2)}) collective-permute-start(bf16[24,1536]{1,0:T(8,128)(2,1)S(1)} %get-tuple-element.30), channel_id=1, source_target_pairs={{0,12},{2,14},{4,0},{6,2},{8,4},{10,6},{12,8},{14,10},{1,13},{3,15... | collective-permute-start | bytes 221192 | tf_op jit(solution)/shard_map/ppermute | solution.py:132
  87.6 1.5 %collective-permute-start.13 = (bf16[24,1536]{1,0:T(8,128)(2,1)S(1)}, bf16[24,1536]{1,0:T(8,128)(2,1)S(1)}, u32[]{:S(2)}, u32[]{:S(2)}) collective-permute-start(bf16[24,1536]{1,0:T(8,128)(2,1)S(1)} %get-tuple-element.29), channel_id=1, source_target_pairs={{0,8},{2,10},{4,12},{6,14},{8,0},{10,2},{12,4},{14,6},{1,9},{3,11}... | collective-permute-start | bytes 221192 | tf_op jit(solution)/shard_map/ppermute | solution.py:132
  89.0 1.8 %collective-permute-done.16 = bf16[96,1536]{1,0:T(8,128)(2,1)S(1)} collective-permute-done((bf16[96,1536]{1,0:T(8,128)(2,1)S(1)}, bf16[96,1536]{1,0:T(8,128)(2,1)S(1)}, u32[]{:S(2)}, u32[]{:S(2)}) %collective-permute-start.16) | collective-permute-done | bytes 294944 | tf_op jit(solution)/shard_map/ppermute | solution.py:135
  91.0 5.5 %collective-permute-start.17 = (bf16[24,1536]{1,0:T(8,128)(2,1)S(1)}, bf16[24,1536]{1,0:T(8,128)(2,1)S(1)}, u32[]{:S(2)}, u32[]{:S(2)}) collective-permute-start(bf16[24,1536]{1,0:T(8,128)(2,1)S(1)} %get-tuple-element.34), channel_id=1, source_target_pairs={{0,12},{2,14},{4,0},{6,2},{8,4},{10,6},{12,8},{14,10},{1,13},{3,15... | collective-permute-start | bytes 221192 | tf_op jit(solution)/shard_map/ppermute | solution.py:132
  96.5 1.3 %collective-permute-start.18 = (bf16[24,1536]{1,0:T(8,128)(2,1)S(1)}, bf16[24,1536]{1,0:T(8,128)(2,1)S(1)}, u32[]{:S(2)}, u32[]{:S(2)}) collective-permute-start(bf16[24,1536]{1,0:T(8,128)(2,1)S(1)} %get-tuple-element.33), channel_id=1, source_target_pairs={{0,8},{2,10},{4,12},{6,14},{8,0},{10,2},{12,4},{14,6},{1,9},{3,11}... | collective-permute-start | bytes 221192 | tf_op jit(solution)/shard_map/ppermute | solution.py:132
  98.1 1.0 collective-permute-done.17
  99.2 5.4 %collective-permute-done.18 = bf16[24,1536]{1,0:T(8,128)(2,1)S(1)} collective-permute-done((bf16[24,1536]{1,0:T(8,128)(2,1)S(1)}, bf16[24,1536]{1,0:T(8,128)(2,1)S(1)}, u32[]{:S(2)}, u32[]{:S(2)}) %collective-permute-start.18) | collective-permute-done | bytes 73760 | tf_op jit(solution)/shard_map/ppermute | solution.py:132
  (65 shorter events, 8.6 us)
Async XLA Ops:
  0.0 2.1 %copy-start = (bf16[64,3072]{1,0:T(8,128)(2,1)S(1)}, bf16[64,3072]{1,0:T(8,128)(2,1)}, u32[]{:S(2)}) copy-start(bf16[64,3072]{1,0:T(8,128)(2,1)} %param.6) | copy-start | bytes 1179652
  2.7 8.1 %collective-permute-start.5 = (bf16[24,1536]{1,0:T(8,128)(2,1)S(1)}, bf16[24,1536]{1,0:T(8,128)(2,1)S(1)}, u32[]{:S(2)}, u32[]{:S(2)}) collective-permute-start(bf16[24,1536]{1,0:T(8,128)(2,1)S(1)} %get-tuple-element.22), channel_id=1, source_target_pairs={{0,4},{2,6},{4,8},{6,10},{8,12},{10,14},{12,0},{14,2},{1,5},{3,7},... | collective-permute-start | bytes 221192 | tf_op jit(solution)/shard_map/ppermute | solution.py:132
  5.8 7.9 %collective-permute-start.6 = (bf16[24,1536]{1,0:T(8,128)(2,1)S(1)}, bf16[24,1536]{1,0:T(8,128)(2,1)S(1)}, u32[]{:S(2)}, u32[]{:S(2)}) collective-permute-start(bf16[24,1536]{1,0:T(8,128)(2,1)S(1)} %get-tuple-element.21), channel_id=1, source_target_pairs={{0,8},{2,10},{4,12},{6,14},{8,0},{10,2},{12,4},{14,6},{1,9},{3,11}... | collective-permute-start | bytes 221192 | tf_op jit(solution)/shard_map/ppermute | solution.py:132
  8.4 6.0 %collective-permute-start.7 = (bf16[24,1536]{1,0:T(8,128)(2,1)S(1)}, bf16[24,1536]{1,0:T(8,128)(2,1)S(1)}, u32[]{:S(2)}, u32[]{:S(2)}) collective-permute-start(bf16[24,1536]{1,0:T(8,128)(2,1)S(1)} %get-tuple-element.20), channel_id=1, source_target_pairs={{0,12},{2,14},{4,0},{6,2},{8,4},{10,6},{12,8},{14,10},{1,13},{3,15... | collective-permute-start | bytes 221192 | tf_op jit(solution)/shard_map/ppermute | solution.py:132
  9.7 6.9 %collective-permute-start = (bf16[24,1536]{1,0:T(8,128)(2,1)S(1)}, bf16[24,1536]{1,0:T(8,128)(2,1)S(1)}, u32[]{:S(2)}, u32[]{:S(2)}) collective-permute-start(bf16[24,1536]{1,0:T(8,128)(2,1)S(1)} %get-tuple-element.25), channel_id=1, source_target_pairs={{0,4},{2,6},{4,8},{6,10},{8,12},{10,14},{12,0},{14,2},{1,5},{3,7},... | collective-permute-start | bytes 221192 | tf_op jit(solution)/shard_map/ppermute | solution.py:132
  10.4 9.2 %collective-permute-start.1 = (bf16[24,1536]{1,0:T(8,128)(2,1)S(1)}, bf16[24,1536]{1,0:T(8,128)(2,1)S(1)}, u32[]{:S(2)}, u32[]{:S(2)}) collective-permute-start(bf16[24,1536]{1,0:T(8,128)(2,1)S(1)} %get-tuple-element.24), channel_id=1, source_target_pairs={{0,8},{2,10},{4,12},{6,14},{8,0},{10,2},{12,4},{14,6},{1,9},{3,11}... | collective-permute-start | bytes 221192 | tf_op jit(solution)/shard_map/ppermute | solution.py:132
  10.8 8.8 %collective-permute-start.2 = (bf16[24,1536]{1,0:T(8,128)(2,1)S(1)}, bf16[24,1536]{1,0:T(8,128)(2,1)S(1)}, u32[]{:S(2)}, u32[]{:S(2)}) collective-permute-start(bf16[24,1536]{1,0:T(8,128)(2,1)S(1)} %get-tuple-element.23), channel_id=1, source_target_pairs={{0,12},{2,14},{4,0},{6,2},{8,4},{10,6},{12,8},{14,10},{1,13},{3,15... | collective-permute-start | bytes 221192 | tf_op jit(solution)/shard_map/ppermute | solution.py:132
  14.5 7.8 %collective-permute-start.8 = (bf16[96,1536]{1,0:T(8,128)(2,1)S(1)}, bf16[96,1536]{1,0:T(8,128)(2,1)S(1)}, u32[]{:S(2)}, u32[]{:S(2)}) collective-permute-start(bf16[96,1536]{1,0:T(8,128)(2,1)S(1)} %pad_maximum_fusion.2), channel_id=1, source_target_pairs={{0,2},{2,0},{4,6},{6,4},{8,10},{10,8},{12,14},{14,12},{1,3},{3,1},... | collective-permute-start | bytes 884744 | tf_op jit(solution)/shard_map/ppermute | solution.py:135
  19.7 8.9 %collective-permute-start.3 = (bf16[96,1536]{1,0:T(8,128)(2,1)S(1)}, bf16[96,1536]{1,0:T(8,128)(2,1)S(1)}, u32[]{:S(2)}, u32[]{:S(2)}) collective-permute-start(bf16[96,1536]{1,0:T(8,128)(2,1)S(1)} %pad_maximum_fusion.1), channel_id=1, source_target_pairs={{0,2},{2,0},{4,6},{6,4},{8,10},{10,8},{12,14},{14,12},{1,3},{3,1},... | collective-permute-start | bytes 884744 | tf_op jit(solution)/shard_map/ppermute | solution.py:135
  22.3 6.4 %collective-permute-start.9 = (bf16[192,1536]{1,0:T(8,128)(2,1)S(1)}, bf16[192,1536]{1,0:T(8,128)(2,1)S(1)}, u32[]{:S(2)}, u32[]{:S(2)}) collective-permute-start(bf16[192,1536]{1,0:T(8,128)(2,1)S(1)} %constant_dynamic-update-slice_fusion.5.refs_1_), channel_id=1, source_target_pairs={{0,1},{1,0},{2,3},{3,2},{4,5},{5,4},{6,7},{7,6},{8,9},{9,8},{10,11... | collective-permute-start | bytes 1769480 | tf_op jit(solution)/shard_map/ppermute | solution.py:138
  28.6 16.1 %collective-permute-start.4 = (bf16[192,1536]{1,0:T(8,128)(2,1)S(1)}, bf16[192,1536]{1,0:T(8,128)(2,1)S(1)}, u32[]{:S(2)}, u32[]{:S(2)}) collective-permute-start(bf16[192,1536]{1,0:T(8,128)(2,1)S(1)} %constant_dynamic-update-slice_fusion.refs_1_), channel_id=1, source_target_pairs={{0,1},{1,0},{2,3},{3,2},{4,5},{5,4},{6,7},{7,6},{8,9},{9,8},{10,11... | collective-permute-start | bytes 1769480 | tf_op jit(solution)/shard_map/ppermute | solution.py:138
  60.7 5.0 %copy-start.2 = (s32[64,2]{0,1:T(2,128)S(1)}, s32[64,2]{0,1:T(2,128)}, u32[]{:S(2)}) copy-start(s32[64,2]{0,1:T(2,128)} %param.8) | copy-start | bytes 1540
  65.1 5.3 %collective-permute-start.10 = (bf16[192,1536]{1,0:T(8,128)(2,1)S(1)}, bf16[192,1536]{1,0:T(8,128)(2,1)S(1)}, u32[]{:S(2)}, u32[]{:S(2)}) collective-permute-start(bf16[192,1536]{1,0:T(8,128)(2,1)S(1)} %shard_map.66), channel_id=1, source_target_pairs={{0,1},{1,0},{2,3},{3,2},{4,5},{5,4},{6,7},{7,6},{8,9},{9,8},{10,11... | collective-permute-start | bytes 1769480 | tf_op jit(solution)/shard_map/ppermute | solution.py:138
  70.5 10.6 %collective-permute-start.11 = (bf16[96,1536]{1,0:T(8,128)(2,1)S(1)}, bf16[96,1536]{1,0:T(8,128)(2,1)S(1)}, u32[]{:S(2)}, u32[]{:S(2)}) collective-permute-start(bf16[96,1536]{1,0:T(8,128)(2,1)S(1)} %slice.119), channel_id=1, source_target_pairs={{0,2},{2,0},{4,6},{6,4},{8,10},{10,8},{12,14},{14,12},{1,3},{3,1},... | collective-permute-start | bytes 884744 | tf_op jit(solution)/shard_map/ppermute | solution.py:135
  76.7 4.6 %collective-permute-start.15 = (bf16[192,1536]{1,0:T(8,128)(2,1)S(1)}, bf16[192,1536]{1,0:T(8,128)(2,1)S(1)}, u32[]{:S(2)}, u32[]{:S(2)}) collective-permute-start(bf16[192,1536]{1,0:T(8,128)(2,1)S(1)} %shard_map.68), channel_id=1, source_target_pairs={{0,1},{1,0},{2,3},{3,2},{4,5},{5,4},{6,7},{7,6},{8,9},{9,8},{10,11... | collective-permute-start | bytes 1769480 | tf_op jit(solution)/shard_map/ppermute | solution.py:138
  81.4 9.5 %collective-permute-start.16 = (bf16[96,1536]{1,0:T(8,128)(2,1)S(1)}, bf16[96,1536]{1,0:T(8,128)(2,1)S(1)}, u32[]{:S(2)}, u32[]{:S(2)}) collective-permute-start(bf16[96,1536]{1,0:T(8,128)(2,1)S(1)} %slice.125), channel_id=1, source_target_pairs={{0,2},{2,0},{4,6},{6,4},{8,10},{10,8},{12,14},{14,12},{1,3},{3,1},... | collective-permute-start | bytes 884744 | tf_op jit(solution)/shard_map/ppermute | solution.py:135
  82.2 15.6 %collective-permute-start.12 = (bf16[24,1536]{1,0:T(8,128)(2,1)S(1)}, bf16[24,1536]{1,0:T(8,128)(2,1)S(1)}, u32[]{:S(2)}, u32[]{:S(2)}) collective-permute-start(bf16[24,1536]{1,0:T(8,128)(2,1)S(1)} %get-tuple-element.30), channel_id=1, source_target_pairs={{0,12},{2,14},{4,0},{6,2},{8,4},{10,6},{12,8},{14,10},{1,13},{3,15... | collective-permute-start | bytes 221192 | tf_op jit(solution)/shard_map/ppermute | solution.py:132
  87.6 10.2 %collective-permute-start.13 = (bf16[24,1536]{1,0:T(8,128)(2,1)S(1)}, bf16[24,1536]{1,0:T(8,128)(2,1)S(1)}, u32[]{:S(2)}, u32[]{:S(2)}) collective-permute-start(bf16[24,1536]{1,0:T(8,128)(2,1)S(1)} %get-tuple-element.29), channel_id=1, source_target_pairs={{0,8},{2,10},{4,12},{6,14},{8,0},{10,2},{12,4},{14,6},{1,9},{3,11}... | collective-permute-start | bytes 221192 | tf_op jit(solution)/shard_map/ppermute | solution.py:132
  89.0 8.8 %collective-permute-start.14 = (bf16[24,1536]{1,0:T(8,128)(2,1)S(1)}, bf16[24,1536]{1,0:T(8,128)(2,1)S(1)}, u32[]{:S(2)}, u32[]{:S(2)}) collective-permute-start(bf16[24,1536]{1,0:T(8,128)(2,1)S(1)} %get-tuple-element.28), channel_id=1, source_target_pairs={{0,4},{2,6},{4,8},{6,10},{8,12},{10,14},{12,0},{14,2},{1,5},{3,7},... | collective-permute-start | bytes 221192 | tf_op jit(solution)/shard_map/ppermute | solution.py:132
  91.0 8.2 %collective-permute-start.17 = (bf16[24,1536]{1,0:T(8,128)(2,1)S(1)}, bf16[24,1536]{1,0:T(8,128)(2,1)S(1)}, u32[]{:S(2)}, u32[]{:S(2)}) collective-permute-start(bf16[24,1536]{1,0:T(8,128)(2,1)S(1)} %get-tuple-element.34), channel_id=1, source_target_pairs={{0,12},{2,14},{4,0},{6,2},{8,4},{10,6},{12,8},{14,10},{1,13},{3,15... | collective-permute-start | bytes 221192 | tf_op jit(solution)/shard_map/ppermute | solution.py:132
  96.5 8.0 %collective-permute-start.18 = (bf16[24,1536]{1,0:T(8,128)(2,1)S(1)}, bf16[24,1536]{1,0:T(8,128)(2,1)S(1)}, u32[]{:S(2)}, u32[]{:S(2)}) collective-permute-start(bf16[24,1536]{1,0:T(8,128)(2,1)S(1)} %get-tuple-element.33), channel_id=1, source_target_pairs={{0,8},{2,10},{4,12},{6,14},{8,0},{10,2},{12,4},{14,6},{1,9},{3,11}... | collective-permute-start | bytes 221192 | tf_op jit(solution)/shard_map/ppermute | solution.py:132
  97.8 6.8 %collective-permute-start.19 = (bf16[24,1536]{1,0:T(8,128)(2,1)S(1)}, bf16[24,1536]{1,0:T(8,128)(2,1)S(1)}, u32[]{:S(2)}, u32[]{:S(2)}) collective-permute-start(bf16[24,1536]{1,0:T(8,128)(2,1)S(1)} %get-tuple-element.32), channel_id=1, source_target_pairs={{0,4},{2,6},{4,8},{6,10},{8,12},{10,14},{12,0},{14,2},{1,5},{3,7},... | collective-permute-start | bytes 221192 | tf_op jit(solution)/shard_map/ppermute | solution.py:132
  97.8 7.8 %copy-start.1 = (bf16[64,3072]{1,0:T(8,128)(2,1)S(1)}, bf16[64,3072]{1,0:T(8,128)(2,1)}, u32[]{:S(2)}) copy-start(bf16[64,3072]{1,0:T(8,128)(2,1)} %param.6) | copy-start | bytes 1179652
